TPU v7x, 32 devices: a whole 2x2x4 slice. The times are simulated.
32 devices in a mesh: dp: 16 (over z, x, core), seq: 2 (over y).
Axes of the slice: x: 2, y: 2, z: 4, core: 2. Of those that a mesh axis runs over, the one named last changes fastest.
Arguments:
- queries: bfloat16 [4096, 4096], P(('dp', 'seq')), may hold values from -6 to 6
- keys: bfloat16 [4096, 512], P(('dp', 'seq')), may hold values from -6 to 6
- values: bfloat16 [4096, 512], P(('dp', 'seq')), may hold values from -6 to 6
- grad_out: bfloat16 [4096, 4096], P(('dp', 'seq')), may hold values from -6 to 6
- quant_scale: float32 [2, 4, 128], replicated, may hold values from 2 to 8
- doc_lengths: int32 [16, 8], P('dp'), may hold values from 1 to 128, as said below
Outputs:
- attn_out: bfloat16 [4096, 4096], P(('dp', 'seq'))
- grad_queries: bfloat16 [4096, 4096], P(('dp', 'seq'))
- grad_keys: bfloat16 [4096, 512], P(('dp', 'seq'))
- grad_values: bfloat16 [4096, 512], P(('dp', 'seq'))
- grad_scale: float32 [2, 4, 128], replicated
Inputs may be any that keep to these rules, and one draw needn't show every extreme that they name: `doc_lengths`: each row sums to 256; its largest length is exactly 128.
All inputs are finite; a program needn't handle non-finite values.
Results may differ from a plain program's by a relative error of at most 0.04.
Values may be sent and summed in bfloat16 or wider, within the bound.
No kernel may reach another device: no remote copies, remote signals or barrier semaphores. Data moves between devices by JAX's collectives and lax.ppermute only.
A program may use at most 64 MiB of HBM per device.

v0:
```python
import functools
import math

import jax
import jax.numpy as jnp
from jax import lax
from jax.experimental import pallas as pl
from jax.experimental.pallas import tpu as pltpu
from jax.sharding import PartitionSpec as P

F32 = jnp.float32
BF16 = jnp.bfloat16
LEVELS = 127.0
NEG = -1e30


def sin_cos_half(u):
    r = (u - jnp.round(u)) * math.pi
    z = r * r
    s = z * (1.0 / 6227020800.0) - 1.0 / 39916800.0
    for c in (1.0 / 362880.0, -1.0 / 5040.0, 1.0 / 120.0, -1.0 / 6.0, 1.0):
        s = s * z + c
    s = s * r
    k = z * (1.0 / 479001600.0) - 1.0 / 3628800.0
    for c in (1.0 / 40320.0, -1.0 / 720.0, 1.0 / 24.0, -0.5, 1.0):
        k = k * z + c
    return s, k


def quant_parts(x, clip):
    inv = 1.0 / clip
    ratio = x * inv
    t = jnp.tanh(ratio)
    u = LEVELS * t
    s, k = sin_cos_half(u)
    level = u - s * k * (1.0 / math.pi)
    unit = level * (1.0 / LEVELS)
    slope = (2.0 * s * s) * (1.0 - t * t)
    return clip * unit, slope, unit - slope * ratio


def prep_kernel(nb, q_hbm, g_hbm, key_hbm, value_hbm, clip_hbm, len_hbm, qt_ref, gt_ref, quant_ref, slope_hbm,
                dclip_ref, bias_ref, clip_out, q_ref, g_ref, key_ref, value_ref, len_ref, slope_ref, sems):
    small = [
        pltpu.make_async_copy(src, dst, sems.at[i])
        for i, (src, dst) in enumerate(
            ((len_hbm, len_ref), (clip_hbm, clip_out), (key_hbm, key_ref), (value_hbm, value_ref))
        )
    ]
    large = [
        pltpu.make_async_copy(q_hbm, q_ref, sems.at[4]),
        pltpu.make_async_copy(g_hbm, g_ref, sems.at[5]),
    ]
    for copy in small + large:
        copy.start()
    rows = key_ref.shape[0]
    kv_heads, hd = clip_out.shape[1], clip_out.shape[2]
    group = q_ref.shape[1] // kv_heads
    base = lax.axis_index("seq") * rows
    for copy in small:
        copy.wait()
    for side, src in ((0, key_ref), (1, value_ref)):
        for n in range(kv_heads):
            x = src[:, n * hd:(n + 1) * hd].astype(F32)
            q, slope, dclip = quant_parts(x, clip_out[side, n:n + 1, :])
            at = slice((side * kv_heads + n) * hd, (side * kv_heads + n + 1) * hd)
            quant_ref[:, at] = q.astype(BF16)
            slope_ref[:, at] = slope
            dclip_ref[:, at] = dclip
    slope_copy = pltpu.make_async_copy(slope_ref, slope_hbm, sems.at[6])
    slope_copy.start()
    key = lax.broadcasted_iota(jnp.int32, (rows, rows), 0)
    row = lax.broadcasted_iota(jnp.int32, (rows, rows), 1)
    start = jnp.zeros((rows, rows), jnp.int32)
    end = jnp.int32(0)
    for d in range(len_ref.shape[1]):
        end = end + len_ref[0, d]
        start = jnp.where(row + base >= end, end, start)
    for b in range(nb):
        pos = jnp.where(key <= row, key, key - nb * rows) if b == 0 else key - b * rows
        bias_ref[b * rows:(b + 1) * rows, :] = jnp.where(pos + base >= start, 0.0, NEG)
    for copy, src, dst in zip(large, (q_ref, g_ref), (qt_ref, gt_ref)):
        copy.wait()
        for n in range(kv_heads):
            for h in range(group // hd):
                at = n * group + h * hd
                dst[n * hd:(n + 1) * hd, h * rows:(h + 1) * rows] = src[:, at:at + hd].T
    slope_copy.wait()


ACROSS = (((1,), (1,)), ((), ()))


def far_order(nb):
    return [nb] + list(range(1, nb))


def near_mask(rows):
    key = lax.broadcasted_iota(jnp.int32, (rows, rows), 0)
    row = lax.broadcasted_iota(jnp.int32, (rows, rows), 1)
    return key <= row


def merge(near, x, nb):
    rows = near.shape[0]
    first = jnp.where(near, x[:rows], x[rows:2 * rows])
    return jnp.concatenate([first, x[2 * rows:]], axis=0) if nb > 1 else first


def split(near_b, far_b, x, nb):
    rows = near_b.shape[0]
    parts = [x[:rows] * near_b, x[:rows] * far_b]
    if nb > 1:
        parts.append(x[rows:])
    return jnp.concatenate(parts, axis=0)


def score_kernel(nb, qt_ref, quant_ref, bias_ref, clip_ref, *rest):
    far, (p_ref, k2_ref, dclip_ref) = rest[:nb], rest[nb:]
    kv_heads, hd = clip_ref.shape[1], clip_ref.shape[2]
    rows, span = bias_ref.shape[1], qt_ref.shape[1]
    factor = hd ** -0.5 * math.log2(math.e)
    near = near_mask(rows)

    bias = bias_ref[...]

    def scores(n):
        cols = slice(n * hd, (n + 1) * hd)
        ks = [quant_ref[:, cols]]
        for j, d in enumerate(far_order(nb)):
            q, _, dclip = quant_parts(far[d - 1][:, cols].astype(F32), clip_ref[0, n:n + 1, :])
            ks.append(q.astype(BF16))
            dclip_ref[j * rows:(j + 1) * rows, cols] = dclip
        k2 = jnp.concatenate(ks, axis=0)
        k2_ref[:, cols] = k2
        return jnp.dot(k2, qt_ref[cols, :], preferred_element_type=F32)

    ahead = scores(0)
    for n in range(kv_heads):
        s_all, ahead = ahead, scores(n + 1) if n + 1 < kv_heads else None
        for h in range(span // rows):
            s = merge(near, s_all[:, h * rows:(h + 1) * rows], nb) * factor + bias
            w = jnp.exp2(s - jnp.max(s, axis=0, keepdims=True))
            p = w * (1.0 / jnp.sum(w, axis=0, keepdims=True))
            p_ref[:, n * span + h * rows:n * span + (h + 1) * rows] = p.astype(BF16)


def grad_kernel(nb, qt_ref, gt_ref, quant_ref, dclip_ref, clip_ref, p_ref, kdclip_ref, *rest):
    far_v, (ds_ref, v2_ref, grad_ref, far_ref, spread_ref, scale_ref) = rest[:nb], rest[nb:]
    kv_heads, hd = clip_ref.shape[1], clip_ref.shape[2]
    rows, span = dclip_ref.shape[0], gt_ref.shape[1]
    heads = span // rows
    width = kv_heads * hd
    scale = hd ** -0.5
    near = near_mask(rows)
    near_b = near.astype(F32).astype(BF16)
    far_b = 1.0 - near_b

    def k_cols(n):
        return slice(n * hd, (n + 1) * hd)

    def v_cols(n):
        return slice(width + n * hd, width + (n + 1) * hd)

    def value_side(n):
        p2 = jnp.concatenate(
            [split(near_b, far_b, p_ref[:, n * span + h * rows:n * span + (h + 1) * rows], nb) for h in range(heads)],
            axis=1,
        )
        v_grad = lax.dot_general(gt_ref[k_cols(n), :], p2, ACROSS, preferred_element_type=F32).T
        vs, vd = [quant_ref[:, v_cols(n)]], [dclip_ref[:, v_cols(n)]]
        for d in far_order(nb):
            q, _, dc = quant_parts(far_v[d - 1][:, k_cols(n)].astype(F32), clip_ref[1, n:n + 1, :])
            vs.append(q.astype(BF16))
            vd.append(dc)
        v2 = jnp.concatenate(vs, axis=0)
        v2_ref[:, k_cols(n)] = v2
        grad_ref[:, v_cols(n)] = v_grad[:rows].astype(BF16)
        far_ref[:, v_cols(n)] = v_grad[rows:].astype(BF16)
        scale_ref[kv_heads + n:kv_heads + n + 1, :] = jnp.sum(
            v_grad * jnp.concatenate(vd, axis=0), axis=0, keepdims=True
        )
        return jnp.dot(v2, gt_ref[k_cols(n), :], preferred_element_type=F32)

    def score_side(n, d_all):
        ds = []
        for h in range(heads):
            dp = merge(near, d_all[:, h * rows:(h + 1) * rows], nb)
            at = slice(n * span + h * rows, n * span + (h + 1) * rows)
            p = p_ref[:, at].astype(F32)
            delta = jnp.sum(p * dp, axis=0, keepdims=True)
            ds_b = (p * (dp - delta)).astype(BF16)
            ds_ref[:, at] = ds_b
            ds.append(split(near_b, far_b, ds_b, nb))
        return jnp.concatenate(ds, axis=1)

    def key_side(n, ds2):
        k_grad = (lax.dot_general(qt_ref[k_cols(n), :], ds2, ACROSS, preferred_element_type=F32) * scale).T
        grad_ref[:, k_cols(n)] = k_grad[:rows].astype(BF16)
        far_ref[:, k_cols(n)] = k_grad[rows:].astype(BF16)
        scale_ref[n:n + 1, :] = jnp.sum(k_grad[:rows] * dclip_ref[:, k_cols(n)], axis=0, keepdims=True) + jnp.sum(
            k_grad[rows:] * kdclip_ref[:, k_cols(n)], axis=0, keepdims=True
        )

    ahead, behind = value_side(0), None
    for n in range(kv_heads):
        d_all, ahead = ahead, value_side(n + 1) if n + 1 < kv_heads else None
        ds2 = score_side(n, d_all)
        if behind is not None:
            key_side(n - 1, behind)
        behind = ds2
    key_side(kv_heads - 1, behind)
    part = scale_ref[...].astype(BF16)

    def spread(i, carry):
        spread_ref[i] = part
        return carry

    lax.fori_loop(0, spread_ref.shape[0], spread, 0, unroll=8)


def output_kernel(nb, p_ref, ds_ref, k2_ref, v2_ref, grad_ref, slope_hbm, *rest):
    backs, rest = rest[:nb], rest[nb:]
    out_hbm, gq_hbm, gk_hbm, gv_hbm, out_ref, gq_ref, gk_ref, gv_ref, slope_ref, back_ref, sems, more_sems = rest
    loads = [pltpu.make_async_copy(slope_hbm, slope_ref, more_sems.at[2])]
    loads += [pltpu.make_async_copy(back, back_ref.at[d], more_sems.at[3 + d]) for d, back in enumerate(backs)]
    for copy in loads:
        copy.start()
    kv_heads = sems.shape[1]
    rows, group = out_ref.shape[0], out_ref.shape[1] // kv_heads
    hd = k2_ref.shape[1] // kv_heads
    heads = group // hd
    near_b = near_mask(rows).astype(F32).astype(BF16)
    far_b = 1.0 - near_b

    def copies(n):
        cols = pl.ds(pl.multiple_of(n * group, group), group)
        return (
            pltpu.make_async_copy(out_ref.at[:, cols], out_hbm.at[:, cols], sems.at[0, n]),
            pltpu.make_async_copy(gq_ref.at[:, cols], gq_hbm.at[:, cols], sems.at[1, n]),
        )

    def step(n, carry):
        cols = pl.ds(pl.multiple_of(n * hd, hd), hd)
        for left, right, dst, scale in ((v2_ref, p_ref, out_ref, None), (k2_ref, ds_ref, gq_ref, hd ** -0.5)):
            at = pl.ds(pl.multiple_of(n * heads * rows, rows), heads * rows)
            x = right[:, at]
            x2 = jnp.concatenate(
                [split(near_b, far_b, x[:, h * rows:(h + 1) * rows], nb) for h in range(heads)], axis=1
            )
            y = jnp.dot(left[:, cols].T, x2, preferred_element_type=F32)
            y = (y if scale is None else y * scale).astype(BF16)
            for h in range(heads):
                dst[:, pl.ds(pl.multiple_of(n * group + h * hd, hd), hd)] = y[:, h * rows:(h + 1) * rows].T
        for copy in copies(n):
            copy.start()
        return carry

    lax.fori_loop(0, kv_heads, step, 0, unroll=True)
    for copy in loads:
        copy.wait()
    stores = []
    width = gk_ref.shape[1]
    for side, ref, dst in ((0, gk_ref, gk_hbm), (1, gv_ref, gv_hbm)):
        at = slice(side * width, (side + 1) * width)
        total = grad_ref[:, at].astype(F32)
        for d in range(nb):
            total = total + back_ref[d, :, at].astype(F32)
        ref[...] = (total * slope_ref[:, at]).astype(BF16)
        stores.append(pltpu.make_async_copy(ref, dst, more_sems.at[side]))
        stores[-1].start()
    for n in range(kv_heads):
        for copy in copies(n):
            copy.wait()
    for copy in stores:
        copy.wait()


def total_kernel(parts_ref, after_ref, out_ref):
    del after_ref
    out_ref[...] = jnp.sum(parts_ref[...].astype(F32), axis=0)


def on_device(sizes, queries, keys, values, grad_out, quant_scale, doc_lengths):
    dp_count, seq_count = sizes
    count = dp_count * seq_count
    nb = max(1, seq_count // 2)
    rows, width = keys.shape
    kv_heads, hd = quant_scale.shape[1], quant_scale.shape[2]
    heads = queries.shape[1] // hd
    vmem = pl.BlockSpec(memory_space=pltpu.VMEM)
    hbm = pl.BlockSpec(memory_space=pltpu.HBM)
    params = pltpu.CompilerParams(vmem_limit_bytes=36 * 1024 * 1024)
    shape = jax.ShapeDtypeStruct
    work = rows * rows * queries.shape[1]

    def call(kernel, name, flops, args, outs, in_specs=None, out_specs=None, scratch=()):
        return pl.pallas_call(
            kernel,
            out_shape=outs,
            in_specs=in_specs or [vmem] * len(args),
            out_specs=out_specs or (vmem,) * len(outs),
            scratch_shapes=scratch,
            compiler_params=params,
            cost_estimate=pl.CostEstimate(flops=flops, bytes_accessed=16 * rows * width, transcendentals=0),
            name=name,
        )(*args)

    def shift(array, d):
        return lax.ppermute(array, "seq", [(r, (r + d) % seq_count) for r in range(seq_count)])

    def unshift(array, d):
        return lax.ppermute(array, "seq", [((r + d) % seq_count, r) for r in range(seq_count)])

    far_k = [shift(keys, d) for d in range(1, nb + 1)]
    far_v = [shift(values, d) for d in range(1, nb + 1)]

    raw = (queries, grad_out, keys, values, quant_scale, doc_lengths)
    qt, gt, quants, slopes, dclips, bias, clips = call(
        functools.partial(prep_kernel, nb),
        "prep",
        2 * work,
        [pltpu.with_memory_space_constraint(x, pltpu.HBM) for x in raw],
        (
            shape((width, heads // kv_heads * rows), BF16),
            shape((width, heads // kv_heads * rows), BF16),
            shape((rows, 2 * width), BF16),
            pltpu.HBM((rows, 2 * width), F32),
            shape((rows, 2 * width), F32),
            shape((nb * rows, rows), F32),
            shape(quant_scale.shape, F32),
        ),
        in_specs=[hbm] * 6,
        out_specs=(vmem, vmem, vmem, hbm, vmem, vmem, vmem),
        scratch=[
            pltpu.VMEM(queries.shape, BF16),
            pltpu.VMEM(queries.shape, BF16),
            pltpu.VMEM(keys.shape, BF16),
            pltpu.VMEM(values.shape, BF16),
            pltpu.SMEM(doc_lengths.shape, jnp.int32),
            pltpu.VMEM((rows, 2 * width), F32),
            pltpu.SemaphoreType.DMA((7,)),
        ],
    )
    p, k2, kdclips = call(
        functools.partial(score_kernel, nb),
        "score",
        2 * (nb + 1) * work,
        (qt, quants, bias, clips, *far_k),
        (
            shape((nb * rows, heads * rows), BF16),
            shape(((nb + 1) * rows, width), BF16),
            shape((nb * rows, width), F32),
        ),
    )
    ds, v2, grads, far_grads, spread = call(
        functools.partial(grad_kernel, nb),
        "grad",
        6 * (nb + 1) * work,
        (qt, gt, quants, dclips, clips, p, kdclips, *far_v),
        (
            shape((nb * rows, heads * rows), BF16),
            shape(((nb + 1) * rows, width), BF16),
            shape((rows, 2 * width), BF16),
            shape((nb * rows, 2 * width), BF16),
            pltpu.VMEM((count, 2 * kv_heads, hd), BF16),
        ),
        scratch=[pltpu.VMEM((2 * kv_heads, hd), F32)],
    )
    backs = []
    for d in range(1, nb + 1):
        at = far_order(nb).index(d) * rows
        backs.append(unshift(lax.slice_in_dim(far_grads, at, at + rows, axis=0), d))
    parts = lax.all_to_all(
        spread,
        ("dp", "seq"),
        split_axis=0,
        concat_axis=0,
        axis_index_groups=[list(reversed(range(count)))],
        tiled=True,
    )
    pinned = pltpu.with_memory_space_constraint(slopes, pltpu.HBM)
    attn_out, grad_queries, grad_keys, grad_values = call(
        functools.partial(output_kernel, nb),
        "output",
        4 * (nb + 1) * work,
        (p, ds, k2, v2, grads, pinned, *backs),
        (
            shape(queries.shape, BF16),
            shape(queries.shape, BF16),
            shape((rows, width), BF16),
            shape((rows, width), BF16),
        ),
        in_specs=[vmem] * 5 + [hbm] + [pl.BlockSpec(memory_space=pl.ANY)] * nb,
        out_specs=(hbm,) * 4,
        scratch=[
            pltpu.VMEM(queries.shape, BF16),
            pltpu.VMEM(queries.shape, BF16),
            pltpu.VMEM((rows, width), BF16),
            pltpu.VMEM((rows, width), BF16),
            pltpu.VMEM((rows, 2 * width), F32),
            pltpu.VMEM((nb, rows, 2 * width), BF16),
            pltpu.SemaphoreType.DMA((2, kv_heads)),
            pltpu.SemaphoreType.DMA((3 + nb,)),
        ],
    )
    (grad_scale,) = call(
        total_kernel,
        "total",
        parts.size,
        (parts, pltpu.with_memory_space_constraint(grad_keys, pltpu.HBM)),
        (shape(parts.shape[1:], F32),),
        in_specs=[vmem, hbm],
    )
    return (attn_out, grad_queries, grad_keys, grad_values, grad_scale.reshape(quant_scale.shape))


def solution(mesh):
    rows = P(("dp", "seq"), None)
    return jax.shard_map(
        functools.partial(on_device, (mesh.shape["dp"], mesh.shape["seq"])),
        mesh=mesh,
        in_specs=(rows, rows, rows, rows, P(), P("dp", None)),
        out_specs=(rows, rows, rows, rows, P()),
        check_vma=False,
    )
```

profile of v0, /device:TPU:0, one launch (start us, length us, event | category | flops | bytes accessed | tf_op | source)
XLA Modules:
  0.0 27.5 jit_solution(6371128462278322421)
XLA Ops:
  0.6 3.0 %collective-permute-start = (bf16[128,512]{1,0:T(8,128)(2,1)}, bf16[128,512]{1,0:T(8,128)(2,1)S(1)}, u32[]{:S(2)}, u32[]{:S(2)}) collective-permute-start(bf16[128,512]{1,0:T(8,128)(2,1)} %key_hbm.1), channel_id=1, source_target_pairs={{0,1},{1,0},{2,3},{3,2},{4,5},{5,4},{6,7},{7,6},{8,9},{9,8},{10,11... | collective-permute-start | bytes 393224 | tf_op jit(solution)/shard_map/ppermute | solution.py:310
  3.7 0.1 collective-permute-start.1
  3.7 2.6 %prep.1 = (bf16[512,1024]{1,0:T(8,128)(2,1)S(1)}, bf16[512,1024]{1,0:T(8,128)(2,1)S(1)}, bf16[128,1024]{1,0:T(8,128)(2,1)S(1)}, f32[128,1024]{1,0:T(8,128)}, f32...) custom-call(bf16[128,4096]{1,0:T(8,128)(2,1)} %q_hbm.1, bf16[128,4096]{1,0:T(8,128)(2,1)} %g_hbm.1, ...), custom_call_target="tpu_custom_call" | custom-call | flops 134217728 | bytes 1048576 | tf_op jit(solution)/shard_map/prep/pallas_call | solution.py:298
  6.3 1.9 %collective-permute-done.rest_0_ = bf16[128,512]{1,0:T(8,128)(2,1)S(1)} collective-permute-done((bf16[128,512]{1,0:T(8,128)(2,1)}, bf16[128,512]{1,0:T(8,128)(2,1)S(1)}, u32[]{:S(2)}, u32[]{:S(2)}) %collective-permute-start) | collective-permute-done | bytes 131104 | tf_op jit(solution)/shard_map/ppermute | solution.py:310
  8.2 1.5 %score.1 = (bf16[128,4096]{1,0:T(8,128)(2,1)S(1)}, bf16[256,512]{1,0:T(8,128)(2,1)S(1)}, f32[128,512]{1,0:T(8,128)S(1)}) custom-call(bf16[512,1024]{1,0:T(8,128)(2,1)S(1)} %get-tuple-element.24.qt_ref, bf16[128,1024]{1,0:T(8,128)(2,1)S(1)} %get-tuple-element.25.quant_ref, f32[128,128]{1,0:T(8,128)S(1)} %get-tuple-element.26.bias_ref, ...), custom_call_target="tpu_custom_call" | custom-call | flops 268435456 | bytes 1048576 | tf_op jit(solution)/shard_map/score/pallas_call | solution.py:298
  9.7 0.4 %collective-permute-done.1.rest_0_ = bf16[128,512]{1,0:T(8,128)(2,1)S(1)} collective-permute-done((bf16[128,512]{1,0:T(8,128)(2,1)}, bf16[128,512]{1,0:T(8,128)(2,1)S(1)}, u32[]{:S(2)}, u32[]{:S(2)}) %collective-permute-start.1) | collective-permute-done | bytes 131104 | tf_op jit(solution)/shard_map/ppermute | solution.py:310
  10.2 2.9 %grad.1 = (bf16[128,4096]{1,0:T(8,128)(2,1)S(1)}, bf16[256,512]{1,0:T(8,128)(2,1)S(1)}, bf16[128,1024]{1,0:T(8,128)(2,1)S(1)}, bf16[128,1024]{1,0:T(8,128)(2,1)S(1)}, bf16[32,8,128]{2,1,0:T(8,128)(2,1)}) custom-call(bf16[512,1024]{1,0:T(8,128)(2,1)S(1)} %get-tuple-element.24.qt_ref, bf16[512,1024]{1,0:T(8,128)(2,1)S(1)} %get-tuple-element.29.gt_ref, ...), custom_call_target="tpu_custom_call" | custom-call | flops 805306368 | bytes 1048576 | tf_op jit(solution)/shard_map/grad/pallas_call | solution.py:298
  13.1 1.7 %collective-permute-start.2 = (bf16[128,1024]{1,0:T(8,128)(2,1)S(1)}, bf16[128,1024]{1,0:T(8,128)(2,1)S(1)}, u32[]{:S(2)}, u32[]{:S(2)}) collective-permute-start(bf16[128,1024]{1,0:T(8,128)(2,1)S(1)} %get-tuple-element.37), channel_id=1, source_target_pairs={{1,0},{0,1},{3,2},{2,3},{5,4},{4,5},{7,6},{6,7},{9,8},{8,9},{11,10... | collective-permute-start | bytes 786440 | tf_op jit(solution)/shard_map/ppermute | solution.py:313
  14.8 4.9 %all-to-all-start = ((bf16[32,8,128]{2,1,0:T(8,128)(2,1)}), bf16[32,8,128]{2,1,0:T(8,128)(2,1)S(1)}, u32[]{:S(2)}, u32[]{:S(2)}) async-start(bf16[32,8,128]{2,1,0:T(8,128)(2,1)} %get-tuple-element.42), calls=%async_computation | async-start | bytes 131072 | tf_op jit(solution)/shard_map/all_to_all | solution.py:374
  19.7 0.9 %collective-permute-done.2.rest_0_ = bf16[128,1024]{1,0:T(8,128)(2,1)S(1)} collective-permute-done((bf16[128,1024]{1,0:T(8,128)(2,1)S(1)}, bf16[128,1024]{1,0:T(8,128)(2,1)S(1)}, u32[]{:S(2)}, u32[]{:S(2)}) %collective-permute-start.2) | collective-permute-done | bytes 262176 | tf_op jit(solution)/shard_map/ppermute | solution.py:313
  20.6 2.1 %output.1 = (bf16[128,4096]{1,0:T(8,128)(2,1)}, bf16[128,4096]{1,0:T(8,128)(2,1)}, bf16[128,512]{1,0:T(8,128)(2,1)}, bf16[128,512]{1,0:T(8,128)(2,1)}) custom-call(bf16[128,4096]{1,0:T(8,128)(2,1)S(1)} %get-tuple-element.28.p_ref, bf16[128,4096]{1,0:T(8,128)(2,1)S(1)} %get-tuple-element.32.ds_ref, bf16[256,512]{1,0:T(8,128)(2,1)S(1)} %get-tuple-element.33.k2_ref, ...), custom_call_target="tpu_custom_call" | custom-call | flops 536870912 | bytes 1048576 | tf_op jit(solution)/shard_map/output/pallas_call | solution.py:298
  22.7 4.1 %all-to-all-done.parts_ref = bf16[32,8,128]{2,1,0:T(8,128)(2,1)S(1)} async-done(((bf16[32,8,128]{2,1,0:T(8,128)(2,1)}), bf16[32,8,128]{2,1,0:T(8,128)(2,1)S(1)}, u32[]{:S(2)}, u32[]{:S(2)}) %all-to-all-start) | async-done | bytes 65568 | tf_op jit(solution)/shard_map/all_to_all | solution.py:374
  26.9 0.6 %total.1 = f32[8,128]{1,0:T(8,128)} custom-call(bf16[32,8,128]{2,1,0:T(8,128)(2,1)S(1)} %all-to-all-done.parts_ref, bf16[128,512]{1,0:T(8,128)(2,1)} %get-tuple-element.21.after_ref), custom_call_target="tpu_custom_call" | custom-call | flops 32768 | bytes 1048576 | tf_op jit(solution)/shard_map/total/pallas_call | solution.py:298
Async XLA Ops:
  0.6 7.6 %collective-permute-start = (bf16[128,512]{1,0:T(8,128)(2,1)}, bf16[128,512]{1,0:T(8,128)(2,1)S(1)}, u32[]{:S(2)}, u32[]{:S(2)}) collective-permute-start(bf16[128,512]{1,0:T(8,128)(2,1)} %key_hbm.1), channel_id=1, source_target_pairs={{0,1},{1,0},{2,3},{3,2},{4,5},{5,4},{6,7},{7,6},{8,9},{9,8},{10,11... | collective-permute-start | bytes 393224 | tf_op jit(solution)/shard_map/ppermute | solution.py:310
  3.7 6.5 %collective-permute-start.1 = (bf16[128,512]{1,0:T(8,128)(2,1)}, bf16[128,512]{1,0:T(8,128)(2,1)S(1)}, u32[]{:S(2)}, u32[]{:S(2)}) collective-permute-start(bf16[128,512]{1,0:T(8,128)(2,1)} %value_hbm.1), channel_id=1, source_target_pairs={{0,1},{1,0},{2,3},{3,2},{4,5},{5,4},{6,7},{7,6},{8,9},{9,8},{10,11... | collective-permute-start | bytes 393224 | tf_op jit(solution)/shard_map/ppermute | solution.py:310
  13.1 7.5 %collective-permute-start.2 = (bf16[128,1024]{1,0:T(8,128)(2,1)S(1)}, bf16[128,1024]{1,0:T(8,128)(2,1)S(1)}, u32[]{:S(2)}, u32[]{:S(2)}) collective-permute-start(bf16[128,1024]{1,0:T(8,128)(2,1)S(1)} %get-tuple-element.37), channel_id=1, source_target_pairs={{1,0},{0,1},{3,2},{2,3},{5,4},{4,5},{7,6},{6,7},{9,8},{8,9},{11,10... | collective-permute-start | bytes 786440 | tf_op jit(solution)/shard_map/ppermute | solution.py:313
  14.8 12.0 %all-to-all-start = ((bf16[32,8,128]{2,1,0:T(8,128)(2,1)}), bf16[32,8,128]{2,1,0:T(8,128)(2,1)S(1)}, u32[]{:S(2)}, u32[]{:S(2)}) async-start(bf16[32,8,128]{2,1,0:T(8,128)(2,1)} %get-tuple-element.42), calls=%async_computation | async-start | bytes 131072 | tf_op jit(solution)/shard_map/all_to_all | solution.py:374
where the time goes:
time: 27.7 us; the launch traced here: 27.5 us
  Pallas kernels  9.78 us (35%)
  starting transfers between devices  9.75 us (35%)
  waiting for transfers between devices  7.28 us (26%)
  between operations  0.67 us (2%)
    pallas_call x5, Pallas kernels, call(): pl.pallas_call(kernel, out_shape=outs, in_specs=in_specs or [vmem] * len(...  9.78 us
    all_to_all x1, starting transfers between devices, on_device(): lax.all_to_all(spread, ('dp', 'seq'), split_axis=0, concat_axis=0, axis_i...  4.89 us
    all_to_all x1, waiting for transfers between devices, on_device(): lax.all_to_all(spread, ('dp', 'seq'), split_axis=0, concat_axis=0, axis_i...  4.13 us
    ppermute x2, starting transfers between devices, shift(): lax.ppermute(array, 'seq', [(r, (r + d) % seq_count) for r in range(seq_c...  3.11 us
    ppermute x2, waiting for transfers between devices, shift(): lax.ppermute(array, 'seq', [(r, (r + d) % seq_count) for r in range(seq_c...  2.3 us
    ppermute x1, starting transfers between devices, unshift(): lax.ppermute(array, 'seq', [((r + d) % seq_count, r) for r in range(seq_c...  1.74 us
    ppermute x1, waiting for transfers between devices, unshift(): lax.ppermute(array, 'seq', [((r + d) % seq_count, r) for r in range(seq_c...  0.85 us
  transfers between devices with their start and end apart: 4, of which 4 were waited for; matrix products, arithmetic and copies ran while one was open for 0% of the time, Pallas kernels for 23%

commit v1 on v0

--- a/solution.py
+++ b/solution.py
@@ -39,25 +39,20 @@
     return clip * unit, slope, unit - slope * ratio
 
 
-def prep_kernel(nb, q_hbm, g_hbm, key_hbm, value_hbm, clip_hbm, len_hbm, qt_ref, gt_ref, quant_ref, slope_hbm,
-                dclip_ref, bias_ref, clip_out, q_ref, g_ref, key_ref, value_ref, len_ref, slope_ref, sems):
-    small = [
+def prep_kernel(nb, key_hbm, value_hbm, clip_hbm, len_hbm, quant_ref, slope_hbm, dclip_ref, bias_ref, clip_out,
+                key_ref, value_ref, len_ref, slope_ref, sems):
+    loads = [
         pltpu.make_async_copy(src, dst, sems.at[i])
         for i, (src, dst) in enumerate(
             ((len_hbm, len_ref), (clip_hbm, clip_out), (key_hbm, key_ref), (value_hbm, value_ref))
         )
     ]
-    large = [
-        pltpu.make_async_copy(q_hbm, q_ref, sems.at[4]),
-        pltpu.make_async_copy(g_hbm, g_ref, sems.at[5]),
-    ]
-    for copy in small + large:
+    for copy in loads:
         copy.start()
     rows = key_ref.shape[0]
     kv_heads, hd = clip_out.shape[1], clip_out.shape[2]
-    group = q_ref.shape[1] // kv_heads
     base = lax.axis_index("seq") * rows
-    for copy in small:
+    for copy in loads:
         copy.wait()
     for side, src in ((0, key_ref), (1, value_ref)):
         for n in range(kv_heads):
@@ -67,7 +62,7 @@
             quant_ref[:, at] = q.astype(BF16)
             slope_ref[:, at] = slope
             dclip_ref[:, at] = dclip
-    slope_copy = pltpu.make_async_copy(slope_ref, slope_hbm, sems.at[6])
+    slope_copy = pltpu.make_async_copy(slope_ref, slope_hbm, sems.at[4])
     slope_copy.start()
     key = lax.broadcasted_iota(jnp.int32, (rows, rows), 0)
     row = lax.broadcasted_iota(jnp.int32, (rows, rows), 1)
@@ -79,13 +74,24 @@
     for b in range(nb):
         pos = jnp.where(key <= row, key, key - nb * rows) if b == 0 else key - b * rows
         bias_ref[b * rows:(b + 1) * rows, :] = jnp.where(pos + base >= start, 0.0, NEG)
-    for copy, src, dst in zip(large, (q_ref, g_ref), (qt_ref, gt_ref)):
-        copy.wait()
+    slope_copy.wait()
+
+
+def turn_kernel(kv_heads, q_hbm, g_hbm, qt_ref, gt_ref, q_ref, g_ref, sems):
+    rows, group = q_ref.shape[0], q_ref.shape[1] // kv_heads
+    hd = qt_ref.shape[0] // kv_heads
+    loads = []
+    for side, (src, dst) in enumerate(((q_hbm, q_ref), (g_hbm, g_ref))):
         for n in range(kv_heads):
+            cols = slice(n * group, (n + 1) * group)
+            loads.append(pltpu.make_async_copy(src.at[:, cols], dst.at[:, cols], sems.at[side, n]))
+            loads[-1].start()
+    for side, (src, dst) in enumerate(((q_ref, qt_ref), (g_ref, gt_ref))):
+        for n in range(kv_heads):
+            loads[side * kv_heads + n].wait()
             for h in range(group // hd):
                 at = n * group + h * hd
                 dst[n * hd:(n + 1) * hd, h * rows:(h + 1) * rows] = src[:, at:at + hd].T
-    slope_copy.wait()
 
 
 ACROSS = (((1,), (1,)), ((), ()))
@@ -115,12 +121,14 @@
     return jnp.concatenate(parts, axis=0)
 
 
-def score_kernel(nb, qt_ref, quant_ref, bias_ref, clip_ref, *rest):
-    far, (p_ref, k2_ref, dclip_ref) = rest[:nb], rest[nb:]
+def score_kernel(nb, qt_ref, gt_ref, quant_ref, bias_ref, clip_ref, *rest):
+    far, (p_ref, k2_ref, dclip_ref, vgrad_ref) = rest[:nb], rest[nb:]
     kv_heads, hd = clip_ref.shape[1], clip_ref.shape[2]
     rows, span = bias_ref.shape[1], qt_ref.shape[1]
     factor = hd ** -0.5 * math.log2(math.e)
     near = near_mask(rows)
+    near_b = near.astype(F32).astype(BF16)
+    far_b = 1.0 - near_b
 
     bias = bias_ref[...]
 
@@ -135,17 +143,31 @@
         k2_ref[:, cols] = k2
         return jnp.dot(k2, qt_ref[cols, :], preferred_element_type=F32)
 
-    ahead = scores(0)
-    for n in range(kv_heads):
-        s_all, ahead = ahead, scores(n + 1) if n + 1 < kv_heads else None
+    def softmax(n, s_all):
+        ps = []
         for h in range(span // rows):
             s = merge(near, s_all[:, h * rows:(h + 1) * rows], nb) * factor + bias
             w = jnp.exp2(s - jnp.max(s, axis=0, keepdims=True))
-            p = w * (1.0 / jnp.sum(w, axis=0, keepdims=True))
-            p_ref[:, n * span + h * rows:n * span + (h + 1) * rows] = p.astype(BF16)
-
-
-def grad_kernel(nb, qt_ref, gt_ref, quant_ref, dclip_ref, clip_ref, p_ref, kdclip_ref, *rest):
+            p = (w * (1.0 / jnp.sum(w, axis=0, keepdims=True))).astype(BF16)
+            p_ref[:, n * span + h * rows:n * span + (h + 1) * rows] = p
+            ps.append(split(near_b, far_b, p, nb))
+        return jnp.concatenate(ps, axis=1)
+
+    def value_grad(n, p2):
+        cols = slice(n * hd, (n + 1) * hd)
+        vgrad_ref[:, cols] = lax.dot_general(gt_ref[cols, :], p2, ACROSS, preferred_element_type=F32).T
+
+    ahead, behind = scores(0), None
+    for n in range(kv_heads):
+        s_all, ahead = ahead, scores(n + 1) if n + 1 < kv_heads else None
+        p2 = softmax(n, s_all)
+        if behind is not None:
+            value_grad(n - 1, behind)
+        behind = p2
+    value_grad(kv_heads - 1, behind)
+
+
+def grad_kernel(nb, qt_ref, gt_ref, quant_ref, dclip_ref, clip_ref, p_ref, kdclip_ref, vgrad_ref, *rest):
     far_v, (ds_ref, v2_ref, grad_ref, far_ref, spread_ref, scale_ref) = rest[:nb], rest[nb:]
     kv_heads, hd = clip_ref.shape[1], clip_ref.shape[2]
     rows, span = dclip_ref.shape[0], gt_ref.shape[1]
@@ -163,11 +185,7 @@
         return slice(width + n * hd, width + (n + 1) * hd)
 
     def value_side(n):
-        p2 = jnp.concatenate(
-            [split(near_b, far_b, p_ref[:, n * span + h * rows:n * span + (h + 1) * rows], nb) for h in range(heads)],
-            axis=1,
-        )
-        v_grad = lax.dot_general(gt_ref[k_cols(n), :], p2, ACROSS, preferred_element_type=F32).T
+        v_grad = vgrad_ref[:, k_cols(n)]
         vs, vd = [quant_ref[:, v_cols(n)]], [dclip_ref[:, v_cols(n)]]
         for d in far_order(nb):
             q, _, dc = quant_parts(far_v[d - 1][:, k_cols(n)].astype(F32), clip_ref[1, n:n + 1, :])
@@ -312,52 +330,64 @@
     def unshift(array, d):
         return lax.ppermute(array, "seq", [((r + d) % seq_count, r) for r in range(seq_count)])
 
+    def pinned(*arrays):
+        return [pltpu.with_memory_space_constraint(x, pltpu.HBM) for x in arrays]
+
     far_k = [shift(keys, d) for d in range(1, nb + 1)]
-    far_v = [shift(values, d) for d in range(1, nb + 1)]
-
-    raw = (queries, grad_out, keys, values, quant_scale, doc_lengths)
-    qt, gt, quants, slopes, dclips, bias, clips = call(
+    quants, slopes, dclips, bias, clips = call(
         functools.partial(prep_kernel, nb),
         "prep",
-        2 * work,
-        [pltpu.with_memory_space_constraint(x, pltpu.HBM) for x in raw],
+        100 * rows * width,
+        pinned(keys, values, quant_scale, doc_lengths),
         (
-            shape((width, heads // kv_heads * rows), BF16),
-            shape((width, heads // kv_heads * rows), BF16),
             shape((rows, 2 * width), BF16),
             pltpu.HBM((rows, 2 * width), F32),
             shape((rows, 2 * width), F32),
             shape((nb * rows, rows), F32),
             shape(quant_scale.shape, F32),
         ),
-        in_specs=[hbm] * 6,
-        out_specs=(vmem, vmem, vmem, hbm, vmem, vmem, vmem),
+        in_specs=[hbm] * 4,
+        out_specs=(vmem, hbm, vmem, vmem, vmem),
         scratch=[
-            pltpu.VMEM(queries.shape, BF16),
-            pltpu.VMEM(queries.shape, BF16),
             pltpu.VMEM(keys.shape, BF16),
             pltpu.VMEM(values.shape, BF16),
             pltpu.SMEM(doc_lengths.shape, jnp.int32),
             pltpu.VMEM((rows, 2 * width), F32),
-            pltpu.SemaphoreType.DMA((7,)),
+            pltpu.SemaphoreType.DMA((5,)),
         ],
     )
-    p, k2, kdclips = call(
+    late_values, bias = lax.optimization_barrier((values, bias))
+    far_v = [shift(late_values, d) for d in range(1, nb + 1)]
+    qt, gt = call(
+        functools.partial(turn_kernel, kv_heads),
+        "turn",
+        work,
+        pinned(queries, grad_out),
+        (shape((width, heads // kv_heads * rows), BF16), shape((width, heads // kv_heads * rows), BF16)),
+        in_specs=[hbm] * 2,
+        scratch=[
+            pltpu.VMEM(queries.shape, BF16),
+            pltpu.VMEM(queries.shape, BF16),
+            pltpu.SemaphoreType.DMA((2, kv_heads)),
+        ],
+    )
+    p, k2, kdclips, v_grads = call(
         functools.partial(score_kernel, nb),
         "score",
-        2 * (nb + 1) * work,
-        (qt, quants, bias, clips, *far_k),
+        4 * (nb + 1) * work,
+        (qt, gt, quants, bias, clips, *far_k),
         (
             shape((nb * rows, heads * rows), BF16),
             shape(((nb + 1) * rows, width), BF16),
             shape((nb * rows, width), F32),
+            shape(((nb + 1) * rows, width), F32),
         ),
     )
     ds, v2, grads, far_grads, spread = call(
         functools.partial(grad_kernel, nb),
         "grad",
-        6 * (nb + 1) * work,
-        (qt, gt, quants, dclips, clips, p, kdclips, *far_v),
+        4 * (nb + 1) * work,
+        (qt, gt, quants, dclips, clips, p, kdclips, v_grads, *far_v),
         (
             shape((nb * rows, heads * rows), BF16),
             shape(((nb + 1) * rows, width), BF16),
@@ -379,12 +409,11 @@
         axis_index_groups=[list(reversed(range(count)))],
         tiled=True,
     )
-    pinned = pltpu.with_memory_space_constraint(slopes, pltpu.HBM)
     attn_out, grad_queries, grad_keys, grad_values = call(
         functools.partial(output_kernel, nb),
         "output",
         4 * (nb + 1) * work,
-        (p, ds, k2, v2, grads, pinned, *backs),
+        (p, ds, k2, v2, grads, *pinned(slopes), *backs),
         (
             shape(queries.shape, BF16),
             shape(queries.shape, BF16),
@@ -408,7 +437,7 @@
         total_kernel,
         "total",
         parts.size,
-        (parts, pltpu.with_memory_space_constraint(grad_keys, pltpu.HBM)),
+        (parts, *pinned(grad_keys)),
         (shape(parts.shape[1:], F32),),
         in_specs=[vmem, hbm],
     )

time: 27.7 us -> 27.9 us (level)
  Pallas kernels: 9.78 us -> 11.6 us
  waiting for transfers between devices: 7.28 us -> 5.95 us
  starting transfers between devices: 9.75 us -> 9.47 us
    pallas_call x5 -> x6, Pallas kernels: 9.78 us -> 11.6 us  [call(): pl.pallas_call(kernel, out_shape=outs, in_specs=in_specs or [vmem] * len(...]
    ppermute x2, waiting for transfers between devices: 2.3 us -> 0.97 us  [shift(): lax.ppermute(array, 'seq', [(r, (r + d) % seq_count) for r in range(seq_c...]
    ppermute x1, starting transfers between devices: 1.74 us -> 1.05 us  [unshift(): lax.ppermute(array, 'seq', [((r + d) % seq_count, r) for r in range(seq_c...]
    all_to_all x1, starting transfers between devices: 4.89 us -> 5.31 us  [on_device(): lax.all_to_all(spread, ('dp', 'seq'), split_axis=0, concat_axis=0, axis_i...]
    ppermute x1, waiting for transfers between devices: 0.85 us -> 0.51 us  [unshift(): lax.ppermute(array, 'seq', [((r + d) % seq_count, r) for r in range(seq_c...]
    all_to_all x1, waiting for transfers between devices: 4.13 us -> 4.47 us  [on_device(): lax.all_to_all(spread, ('dp', 'seq'), split_axis=0, concat_axis=0, axis_i...]
  transfers between devices with their start and end apart: 4 -> 4, of which waited for: 4 -> 3; matrix products, arithmetic and copies ran while one was open for 0% -> 0% of each run, Pallas kernels for 23% -> 30%
where the time goes in v1:
time: 27.9 us; the launch traced here: 27.7 us
  Pallas kernels  11.6 us (42%)
  starting transfers between devices  9.47 us (34%)
  waiting for transfers between devices  5.95 us (21%)
  between operations  0.7 us (3%)
    pallas_call x6, Pallas kernels, call(): pl.pallas_call(kernel, out_shape=outs, in_specs=in_specs or [vmem] * len(...  11.6 us
    all_to_all x1, starting transfers between devices, on_device(): lax.all_to_all(spread, ('dp', 'seq'), split_axis=0, concat_axis=0, axis_i...  5.31 us
    all_to_all x1, waiting for transfers between devices, on_device(): lax.all_to_all(spread, ('dp', 'seq'), split_axis=0, concat_axis=0, axis_i...  4.47 us
    ppermute x2, starting transfers between devices, shift(): lax.ppermute(array, 'seq', [(r, (r + d) % seq_count) for r in range(seq_c...  3.11 us
    ppermute x1, starting transfers between devices, unshift(): lax.ppermute(array, 'seq', [((r + d) % seq_count, r) for r in range(seq_c...  1.05 us
    ppermute x2, waiting for transfers between devices, shift(): lax.ppermute(array, 'seq', [(r, (r + d) % seq_count) for r in range(seq_c...  0.97 us
  transfers between devices with their start and end apart: 4, of which 3 were waited for; matrix products, arithmetic and copies ran while one was open for 0% of the time, Pallas kernels for 30%

profile of v1, /device:TPU:0, one launch (start us, length us, event | category | flops | bytes accessed | tf_op | source)
XLA Modules:
  0.0 27.7 jit_solution(13931807156526261114)
XLA Ops:
  0.6 0.0 copy-start
  0.6 3.0 %collective-permute-start = (bf16[128,512]{1,0:T(8,128)(2,1)}, bf16[128,512]{1,0:T(8,128)(2,1)S(1)}, u32[]{:S(2)}, u32[]{:S(2)}) collective-permute-start(bf16[128,512]{1,0:T(8,128)(2,1)} %key_hbm.1), channel_id=1, source_target_pairs={{0,1},{1,0},{2,3},{3,2},{4,5},{5,4},{6,7},{7,6},{8,9},{9,8},{10,11... | collective-permute-start | bytes 393224 | tf_op jit(solution)/shard_map/ppermute | solution.py:328
  3.7 2.3 %prep.1 = (bf16[128,1024]{1,0:T(8,128)(2,1)S(1)}, f32[128,1024]{1,0:T(8,128)}, f32[128,1024]{1,0:T(8,128)S(1)}, f32[128,128]{1,0:T(8,128)S(1)}, f32[2,4,128]{2,1,0:T(4,128)S(1)}) custom-call(bf16[128,512]{1,0:T(8,128)(2,1)} %key_hbm.1, bf16[128,512]{1,0:T(8,128)(2,1)} %value_hbm.1, f32[2,4,128]{2,1,0:T(4,128)} %clip_hbm.1, s32[1,8]{1,0:T(1,128)} %len_hbm.1), custom_call_target="tpu_custom_call" | custom-call | flops 6553600 | bytes 1048576 | tf_op jit(solution)/shard_map/prep/pallas_call | solution.py:316
  6.0 0.0 copy-done
  6.0 0.1 collective-permute-start.1
  6.1 2.0 %turn.1 = (bf16[512,1024]{1,0:T(8,128)(2,1)S(1)}, bf16[512,1024]{1,0:T(8,128)(2,1)S(1)}) custom-call(bf16[128,4096]{1,0:T(8,128)(2,1)} %q_hbm.1, bf16[128,4096]{1,0:T(8,128)(2,1)} %g_hbm.1), custom_call_target="tpu_custom_call" | custom-call | flops 67108864 | bytes 1048576 | tf_op jit(solution)/shard_map/turn/pallas_call | solution.py:316
  8.1 0.0 collective-permute-done.rest_0_
  8.1 1.9 %score.1 = (bf16[128,4096]{1,0:T(8,128)(2,1)S(1)}, bf16[256,512]{1,0:T(8,128)(2,1)S(1)}, f32[128,512]{1,0:T(8,128)S(1)}, f32[256,512]{1,0:T(8,128)S(1)}) custom-call(bf16[512,1024]{1,0:T(8,128)(2,1)S(1)} %get-tuple-element.27.qt_ref, bf16[512,1024]{1,0:T(8,128)(2,1)S(1)} %get-tuple-element.28.gt_ref, bf16[128,1024]{1,0:T(8,128)(2,1)S(1)} %get-tuple-element.29.quant_ref, ...), custom_call_target="tpu_custom_call" | custom-call | flops 536870912 | bytes 1048576 | tf_op jit(solution)/shard_map/score/pallas_call | solution.py:316
  10.1 1.0 %collective-permute-done.1.rest_0_ = bf16[128,512]{1,0:T(8,128)(2,1)S(1)} collective-permute-done((bf16[128,512]{1,0:T(8,128)(2,1)S(1)}, bf16[128,512]{1,0:T(8,128)(2,1)S(1)}, u32[]{:S(2)}, u32[]{:S(2)}) %collective-permute-start.1) | collective-permute-done | bytes 131104 | tf_op jit(solution)/shard_map/ppermute | solution.py:328
  11.0 2.5 %grad.1 = (bf16[128,4096]{1,0:T(8,128)(2,1)S(1)}, bf16[256,512]{1,0:T(8,128)(2,1)S(1)}, bf16[128,1024]{1,0:T(8,128)(2,1)S(1)}, bf16[128,1024]{1,0:T(8,128)(2,1)S(1)}, bf16[32,8,128]{2,1,0:T(8,128)(2,1)}) custom-call(bf16[512,1024]{1,0:T(8,128)(2,1)S(1)} %get-tuple-element.27.qt_ref, bf16[512,1024]{1,0:T(8,128)(2,1)S(1)} %get-tuple-element.28.gt_ref, ...), custom_call_target="tpu_custom_call" | custom-call | flops 536870912 | bytes 1048576 | tf_op jit(solution)/shard_map/grad/pallas_call | solution.py:316
  13.6 1.0 %collective-permute-start.2 = (bf16[128,1024]{1,0:T(8,128)(2,1)S(1)}, bf16[128,1024]{1,0:T(8,128)(2,1)S(1)}, u32[]{:S(2)}, u32[]{:S(2)}) collective-permute-start(bf16[128,1024]{1,0:T(8,128)(2,1)S(1)} %get-tuple-element.43), channel_id=1, source_target_pairs={{1,0},{0,1},{3,2},{2,3},{5,4},{4,5},{7,6},{6,7},{9,8},{8,9},{11,10... | collective-permute-start | bytes 786440 | tf_op jit(solution)/shard_map/ppermute | solution.py:331
  14.6 5.3 %all-to-all-start = ((bf16[32,8,128]{2,1,0:T(8,128)(2,1)}), bf16[32,8,128]{2,1,0:T(8,128)(2,1)S(1)}, u32[]{:S(2)}, u32[]{:S(2)}) async-start(bf16[32,8,128]{2,1,0:T(8,128)(2,1)} %get-tuple-element.48), calls=%async_computation | async-start | bytes 131072 | tf_op jit(solution)/shard_map/all_to_all | solution.py:404
  19.9 0.5 %collective-permute-done.2.rest_0_ = bf16[128,1024]{1,0:T(8,128)(2,1)S(1)} collective-permute-done((bf16[128,1024]{1,0:T(8,128)(2,1)S(1)}, bf16[128,1024]{1,0:T(8,128)(2,1)S(1)}, u32[]{:S(2)}, u32[]{:S(2)}) %collective-permute-start.2) | collective-permute-done | bytes 262176 | tf_op jit(solution)/shard_map/ppermute | solution.py:331
  20.4 2.1 %output.1 = (bf16[128,4096]{1,0:T(8,128)(2,1)}, bf16[128,4096]{1,0:T(8,128)(2,1)}, bf16[128,512]{1,0:T(8,128)(2,1)}, bf16[128,512]{1,0:T(8,128)(2,1)}) custom-call(bf16[128,4096]{1,0:T(8,128)(2,1)S(1)} %get-tuple-element.33.p_ref, bf16[128,4096]{1,0:T(8,128)(2,1)S(1)} %get-tuple-element.38.ds_ref, bf16[256,512]{1,0:T(8,128)(2,1)S(1)} %get-tuple-element.39.k2_ref, ...), custom_call_target="tpu_custom_call" | custom-call | flops 536870912 | bytes 1048576 | tf_op jit(solution)/shard_map/output/pallas_call | solution.py:316
  22.6 4.5 %all-to-all-done.parts_ref = bf16[32,8,128]{2,1,0:T(8,128)(2,1)S(1)} async-done(((bf16[32,8,128]{2,1,0:T(8,128)(2,1)}), bf16[32,8,128]{2,1,0:T(8,128)(2,1)S(1)}, u32[]{:S(2)}, u32[]{:S(2)}) %all-to-all-start) | async-done | bytes 65568 | tf_op jit(solution)/shard_map/all_to_all | solution.py:404
  27.1 0.6 %total.1 = f32[8,128]{1,0:T(8,128)} custom-call(bf16[32,8,128]{2,1,0:T(8,128)(2,1)S(1)} %all-to-all-done.parts_ref, bf16[128,512]{1,0:T(8,128)(2,1)} %get-tuple-element.24.after_ref), custom_call_target="tpu_custom_call" | custom-call | flops 32768 | bytes 1048576 | tf_op jit(solution)/shard_map/total/pallas_call | solution.py:316
Async XLA Ops:
  0.6 5.4 %copy-start = (bf16[128,512]{1,0:T(8,128)(2,1)S(1)}, bf16[128,512]{1,0:T(8,128)(2,1)}, u32[]{:S(2)}) copy-start(bf16[128,512]{1,0:T(8,128)(2,1)} %value_hbm.1) | copy-start | bytes 393220
  0.6 7.5 %collective-permute-start = (bf16[128,512]{1,0:T(8,128)(2,1)}, bf16[128,512]{1,0:T(8,128)(2,1)S(1)}, u32[]{:S(2)}, u32[]{:S(2)}) collective-permute-start(bf16[128,512]{1,0:T(8,128)(2,1)} %key_hbm.1), channel_id=1, source_target_pairs={{0,1},{1,0},{2,3},{3,2},{4,5},{5,4},{6,7},{7,6},{8,9},{9,8},{10,11... | collective-permute-start | bytes 393224 | tf_op jit(solution)/shard_map/ppermute | solution.py:328
  6.0 5.0 %collective-permute-start.1 = (bf16[128,512]{1,0:T(8,128)(2,1)S(1)}, bf16[128,512]{1,0:T(8,128)(2,1)S(1)}, u32[]{:S(2)}, u32[]{:S(2)}) collective-permute-start(bf16[128,512]{1,0:T(8,128)(2,1)S(1)} %copy-done), channel_id=1, source_target_pairs={{0,1},{1,0},{2,3},{3,2},{4,5},{5,4},{6,7},{7,6},{8,9},{9,8},{10,11... | collective-permute-start | bytes 393224 | tf_op jit(solution)/shard_map/ppermute | solution.py:328
  13.6 6.9 %collective-permute-start.2 = (bf16[128,1024]{1,0:T(8,128)(2,1)S(1)}, bf16[128,1024]{1,0:T(8,128)(2,1)S(1)}, u32[]{:S(2)}, u32[]{:S(2)}) collective-permute-start(bf16[128,1024]{1,0:T(8,128)(2,1)S(1)} %get-tuple-element.43), channel_id=1, source_target_pairs={{1,0},{0,1},{3,2},{2,3},{5,4},{4,5},{7,6},{6,7},{9,8},{8,9},{11,10... | collective-permute-start | bytes 786440 | tf_op jit(solution)/shard_map/ppermute | solution.py:331
  14.6 12.4 %all-to-all-start = ((bf16[32,8,128]{2,1,0:T(8,128)(2,1)}), bf16[32,8,128]{2,1,0:T(8,128)(2,1)S(1)}, u32[]{:S(2)}, u32[]{:S(2)}) async-start(bf16[32,8,128]{2,1,0:T(8,128)(2,1)} %get-tuple-element.48), calls=%async_computation | async-start | bytes 131072 | tf_op jit(solution)/shard_map/all_to_all | solution.py:404

commit v2 on v0

--- a/solution.py
+++ b/solution.py
@@ -88,9 +88,6 @@
     slope_copy.wait()
 
 
-ACROSS = (((1,), (1,)), ((), ()))
-
-
 def far_order(nb):
     return [nb] + list(range(1, nb))
 
@@ -145,7 +142,7 @@
             p_ref[:, n * span + h * rows:n * span + (h + 1) * rows] = p.astype(BF16)
 
 
-def grad_kernel(nb, qt_ref, gt_ref, quant_ref, dclip_ref, clip_ref, p_ref, kdclip_ref, *rest):
+def grad_kernel(nb, q_ref, g_ref, gt_ref, quant_ref, dclip_ref, clip_ref, p_ref, kdclip_ref, *rest):
     far_v, (ds_ref, v2_ref, grad_ref, far_ref, spread_ref, scale_ref) = rest[:nb], rest[nb:]
     kv_heads, hd = clip_ref.shape[1], clip_ref.shape[2]
     rows, span = dclip_ref.shape[0], gt_ref.shape[1]
@@ -162,12 +159,17 @@
     def v_cols(n):
         return slice(width + n * hd, width + (n + 1) * hd)
 
+    def stacked(ref, n):
+        return jnp.concatenate(
+            [ref[:, (n * heads + h) * hd:(n * heads + h + 1) * hd] for h in range(heads)], axis=0
+        )
+
     def value_side(n):
         p2 = jnp.concatenate(
             [split(near_b, far_b, p_ref[:, n * span + h * rows:n * span + (h + 1) * rows], nb) for h in range(heads)],
             axis=1,
         )
-        v_grad = lax.dot_general(gt_ref[k_cols(n), :], p2, ACROSS, preferred_element_type=F32).T
+        v_grad = jnp.dot(p2, stacked(g_ref, n), preferred_element_type=F32)
         vs, vd = [quant_ref[:, v_cols(n)]], [dclip_ref[:, v_cols(n)]]
         for d in far_order(nb):
             q, _, dc = quant_parts(far_v[d - 1][:, k_cols(n)].astype(F32), clip_ref[1, n:n + 1, :])
@@ -195,7 +197,7 @@
         return jnp.concatenate(ds, axis=1)
 
     def key_side(n, ds2):
-        k_grad = (lax.dot_general(qt_ref[k_cols(n), :], ds2, ACROSS, preferred_element_type=F32) * scale).T
+        k_grad = jnp.dot(ds2, stacked(q_ref, n), preferred_element_type=F32) * scale
         grad_ref[:, k_cols(n)] = k_grad[:rows].astype(BF16)
         far_ref[:, k_cols(n)] = k_grad[rows:].astype(BF16)
         scale_ref[n:n + 1, :] = jnp.sum(k_grad[:rows] * dclip_ref[:, k_cols(n)], axis=0, keepdims=True) + jnp.sum(
@@ -316,7 +318,7 @@
     far_v = [shift(values, d) for d in range(1, nb + 1)]
 
     raw = (queries, grad_out, keys, values, quant_scale, doc_lengths)
-    qt, gt, quants, slopes, dclips, bias, clips = call(
+    qt, gt, quants, slopes, dclips, bias, clips, q, g = call(
         functools.partial(prep_kernel, nb),
         "prep",
         2 * work,
@@ -329,12 +331,12 @@
             shape((rows, 2 * width), F32),
             shape((nb * rows, rows), F32),
             shape(quant_scale.shape, F32),
+            shape(queries.shape, BF16),
+            shape(queries.shape, BF16),
         ),
         in_specs=[hbm] * 6,
-        out_specs=(vmem, vmem, vmem, hbm, vmem, vmem, vmem),
+        out_specs=(vmem, vmem, vmem, hbm, vmem, vmem, vmem, vmem, vmem),
         scratch=[
-            pltpu.VMEM(queries.shape, BF16),
-            pltpu.VMEM(queries.shape, BF16),
             pltpu.VMEM(keys.shape, BF16),
             pltpu.VMEM(values.shape, BF16),
             pltpu.SMEM(doc_lengths.shape, jnp.int32),
@@ -357,7 +359,7 @@
         functools.partial(grad_kernel, nb),
         "grad",
         6 * (nb + 1) * work,
-        (qt, gt, quants, dclips, clips, p, kdclips, *far_v),
+        (q, g, gt, quants, dclips, clips, p, kdclips, *far_v),
         (
             shape((nb * rows, heads * rows), BF16),
             shape(((nb + 1) * rows, width), BF16),

time: 27.7 us -> 27.9 us (level)
  no operation moved by 1% of the time
where the time goes in v2:
time: 27.9 us; the launch traced here: 27.7 us
  Pallas kernels  10 us (36%)
  starting transfers between devices  9.75 us (35%)
  waiting for transfers between devices  7.29 us (26%)
  between operations  0.67 us (2%)
    pallas_call x5, Pallas kernels, call(): pl.pallas_call(kernel, out_shape=outs, in_specs=in_specs or [vmem] * len(...  10 us
    all_to_all x1, starting transfers between devices, on_device(): lax.all_to_all(spread, ('dp', 'seq'), split_axis=0, concat_axis=0, axis_i...  4.92 us
    all_to_all x1, waiting for transfers between devices, on_device(): lax.all_to_all(spread, ('dp', 'seq'), split_axis=0, concat_axis=0, axis_i...  4.13 us
    ppermute x2, starting transfers between devices, shift(): lax.ppermute(array, 'seq', [(r, (r + d) % seq_count) for r in range(seq_c...  3.11 us
    ppermute x2, waiting for transfers between devices, shift(): lax.ppermute(array, 'seq', [(r, (r + d) % seq_count) for r in range(seq_c...  2.31 us
    ppermute x1, starting transfers between devices, unshift(): lax.ppermute(array, 'seq', [((r + d) % seq_count, r) for r in range(seq_c...  1.72 us
    ppermute x1, waiting for transfers between devices, unshift(): lax.ppermute(array, 'seq', [((r + d) % seq_count, r) for r in range(seq_c...  0.85 us
  transfers between devices with their start and end apart: 4, of which 4 were waited for; matrix products, arithmetic and copies ran while one was open for 0% of the time, Pallas kernels for 23%

profile of v2, /device:TPU:0, one launch (start us, length us, event | category | flops | bytes accessed | tf_op | source)
XLA Modules:
  0.0 27.7 jit_solution(16047582599594430838)
XLA Ops:
  0.6 3.0 %collective-permute-start = (bf16[128,512]{1,0:T(8,128)(2,1)}, bf16[128,512]{1,0:T(8,128)(2,1)S(1)}, u32[]{:S(2)}, u32[]{:S(2)}) collective-permute-start(bf16[128,512]{1,0:T(8,128)(2,1)} %key_hbm.1), channel_id=1, source_target_pairs={{0,1},{1,0},{2,3},{3,2},{4,5},{5,4},{6,7},{7,6},{8,9},{9,8},{10,11... | collective-permute-start | bytes 393224 | tf_op jit(solution)/shard_map/ppermute | solution.py:312
  3.7 0.1 collective-permute-start.1
  3.7 2.6 %prep.1 = (bf16[512,1024]{1,0:T(8,128)(2,1)S(1)}, bf16[512,1024]{1,0:T(8,128)(2,1)S(1)}, bf16[128,1024]{1,0:T(8,128)(2,1)S(1)}, f32[128,1024]{1,0:T(8,128)}, f32...) custom-call(bf16[128,4096]{1,0:T(8,128)(2,1)} %q_hbm.1, ...), custom_call_target="tpu_custom_call" | custom-call | flops 134217728 | bytes 1048576 | tf_op jit(solution)/shard_map/prep/pallas_call | solution.py:300
  6.3 1.9 %collective-permute-done.rest_0_ = bf16[128,512]{1,0:T(8,128)(2,1)S(1)} collective-permute-done((bf16[128,512]{1,0:T(8,128)(2,1)}, bf16[128,512]{1,0:T(8,128)(2,1)S(1)}, u32[]{:S(2)}, u32[]{:S(2)}) %collective-permute-start) | collective-permute-done | bytes 131104 | tf_op jit(solution)/shard_map/ppermute | solution.py:312
  8.2 1.5 %score.1 = (bf16[128,4096]{1,0:T(8,128)(2,1)S(1)}, bf16[256,512]{1,0:T(8,128)(2,1)S(1)}, f32[128,512]{1,0:T(8,128)S(1)}) custom-call(bf16[512,1024]{1,0:T(8,128)(2,1)S(1)} %get-tuple-element.26.qt_ref, bf16[128,1024]{1,0:T(8,128)(2,1)S(1)} %get-tuple-element.27.quant_ref, f32[128,128]{1,0:T(8,128)S(1)} %get-tuple-element.28.bias_ref, ...), custom_call_target="tpu_custom_call" | custom-call | flops 268435456 | bytes 1048576 | tf_op jit(solution)/shard_map/score/pallas_call | solution.py:300
  9.7 0.4 %collective-permute-done.1.rest_0_ = bf16[128,512]{1,0:T(8,128)(2,1)S(1)} collective-permute-done((bf16[128,512]{1,0:T(8,128)(2,1)}, bf16[128,512]{1,0:T(8,128)(2,1)S(1)}, u32[]{:S(2)}, u32[]{:S(2)}) %collective-permute-start.1) | collective-permute-done | bytes 131104 | tf_op jit(solution)/shard_map/ppermute | solution.py:312
  10.2 3.1 %grad.1 = (bf16[128,4096]{1,0:T(8,128)(2,1)S(1)}, bf16[256,512]{1,0:T(8,128)(2,1)S(1)}, bf16[128,1024]{1,0:T(8,128)(2,1)S(1)}, bf16[128,1024]{1,0:T(8,128)(2,1)S(1)}, bf16[32,8,128]{2,1,0:T(8,128)(2,1)}) custom-call(bf16[128,4096]{1,0:T(8,128)(2,1)S(1)} %get-tuple-element.31.q_ref, bf16[128,4096]{1,0:T(8,128)(2,1)S(1)} %get-tuple-element.32.g_ref, ...), custom_call_target="tpu_custom_call" | custom-call | flops 805306368 | bytes 1048576 | tf_op jit(solution)/shard_map/grad/pallas_call | solution.py:300
  13.3 1.7 %collective-permute-start.2 = (bf16[128,1024]{1,0:T(8,128)(2,1)S(1)}, bf16[128,1024]{1,0:T(8,128)(2,1)S(1)}, u32[]{:S(2)}, u32[]{:S(2)}) collective-permute-start(bf16[128,1024]{1,0:T(8,128)(2,1)S(1)} %get-tuple-element.41), channel_id=1, source_target_pairs={{1,0},{0,1},{3,2},{2,3},{5,4},{4,5},{7,6},{6,7},{9,8},{8,9},{11,10... | collective-permute-start | bytes 786440 | tf_op jit(solution)/shard_map/ppermute | solution.py:315
  15.0 4.9 %all-to-all-start = ((bf16[32,8,128]{2,1,0:T(8,128)(2,1)}), bf16[32,8,128]{2,1,0:T(8,128)(2,1)S(1)}, u32[]{:S(2)}, u32[]{:S(2)}) async-start(bf16[32,8,128]{2,1,0:T(8,128)(2,1)} %get-tuple-element.46), calls=%async_computation | async-start | bytes 131072 | tf_op jit(solution)/shard_map/all_to_all | solution.py:376
  20.0 0.9 %collective-permute-done.2.rest_0_ = bf16[128,1024]{1,0:T(8,128)(2,1)S(1)} collective-permute-done((bf16[128,1024]{1,0:T(8,128)(2,1)S(1)}, bf16[128,1024]{1,0:T(8,128)(2,1)S(1)}, u32[]{:S(2)}, u32[]{:S(2)}) %collective-permute-start.2) | collective-permute-done | bytes 262176 | tf_op jit(solution)/shard_map/ppermute | solution.py:315
  20.8 2.1 %output.1 = (bf16[128,4096]{1,0:T(8,128)(2,1)}, bf16[128,4096]{1,0:T(8,128)(2,1)}, bf16[128,512]{1,0:T(8,128)(2,1)}, bf16[128,512]{1,0:T(8,128)(2,1)}) custom-call(bf16[128,4096]{1,0:T(8,128)(2,1)S(1)} %get-tuple-element.30.p_ref, bf16[128,4096]{1,0:T(8,128)(2,1)S(1)} %get-tuple-element.36.ds_ref, bf16[256,512]{1,0:T(8,128)(2,1)S(1)} %get-tuple-element.37.k2_ref, ...), custom_call_target="tpu_custom_call" | custom-call | flops 536870912 | bytes 1048576 | tf_op jit(solution)/shard_map/output/pallas_call | solution.py:300
  23.0 4.1 %all-to-all-done.parts_ref = bf16[32,8,128]{2,1,0:T(8,128)(2,1)S(1)} async-done(((bf16[32,8,128]{2,1,0:T(8,128)(2,1)}), bf16[32,8,128]{2,1,0:T(8,128)(2,1)S(1)}, u32[]{:S(2)}, u32[]{:S(2)}) %all-to-all-start) | async-done | bytes 65568 | tf_op jit(solution)/shard_map/all_to_all | solution.py:376
  27.1 0.6 %total.1 = f32[8,128]{1,0:T(8,128)} custom-call(bf16[32,8,128]{2,1,0:T(8,128)(2,1)S(1)} %all-to-all-done.parts_ref, bf16[128,512]{1,0:T(8,128)(2,1)} %get-tuple-element.23.after_ref), custom_call_target="tpu_custom_call" | custom-call | flops 32768 | bytes 1048576 | tf_op jit(solution)/shard_map/total/pallas_call | solution.py:300
Async XLA Ops:
  0.6 7.6 %collective-permute-start = (bf16[128,512]{1,0:T(8,128)(2,1)}, bf16[128,512]{1,0:T(8,128)(2,1)S(1)}, u32[]{:S(2)}, u32[]{:S(2)}) collective-permute-start(bf16[128,512]{1,0:T(8,128)(2,1)} %key_hbm.1), channel_id=1, source_target_pairs={{0,1},{1,0},{2,3},{3,2},{4,5},{5,4},{6,7},{7,6},{8,9},{9,8},{10,11... | collective-permute-start | bytes 393224 | tf_op jit(solution)/shard_map/ppermute | solution.py:312
  3.7 6.5 %collective-permute-start.1 = (bf16[128,512]{1,0:T(8,128)(2,1)}, bf16[128,512]{1,0:T(8,128)(2,1)S(1)}, u32[]{:S(2)}, u32[]{:S(2)}) collective-permute-start(bf16[128,512]{1,0:T(8,128)(2,1)} %value_hbm.1), channel_id=1, source_target_pairs={{0,1},{1,0},{2,3},{3,2},{4,5},{5,4},{6,7},{7,6},{8,9},{9,8},{10,11... | collective-permute-start | bytes 393224 | tf_op jit(solution)/shard_map/ppermute | solution.py:312
  13.3 7.5 %collective-permute-start.2 = (bf16[128,1024]{1,0:T(8,128)(2,1)S(1)}, bf16[128,1024]{1,0:T(8,128)(2,1)S(1)}, u32[]{:S(2)}, u32[]{:S(2)}) collective-permute-start(bf16[128,1024]{1,0:T(8,128)(2,1)S(1)} %get-tuple-element.41), channel_id=1, source_target_pairs={{1,0},{0,1},{3,2},{2,3},{5,4},{4,5},{7,6},{6,7},{9,8},{8,9},{11,10... | collective-permute-start | bytes 786440 | tf_op jit(solution)/shard_map/ppermute | solution.py:315
  15.0 12.1 %all-to-all-start = ((bf16[32,8,128]{2,1,0:T(8,128)(2,1)}), bf16[32,8,128]{2,1,0:T(8,128)(2,1)S(1)}, u32[]{:S(2)}, u32[]{:S(2)}) async-start(bf16[32,8,128]{2,1,0:T(8,128)(2,1)} %get-tuple-element.46), calls=%async_computation | async-start | bytes 131072 | tf_op jit(solution)/shard_map/all_to_all | solution.py:376

commit v3 on v0

--- a/solution.py
+++ b/solution.py
@@ -312,8 +312,11 @@
     def unshift(array, d):
         return lax.ppermute(array, "seq", [((r + d) % seq_count, r) for r in range(seq_count)])
 
+    def shift_up(array, d):
+        return lax.ppermute(array, "seq", [(r, r + d) for r in range(seq_count - d)])
+
     far_k = [shift(keys, d) for d in range(1, nb + 1)]
-    far_v = [shift(values, d) for d in range(1, nb + 1)]
+    far_v = [shift_up(values, d) for d in range(1, nb + 1)]
 
     raw = (queries, grad_out, keys, values, quant_scale, doc_lengths)
     qt, gt, quants, slopes, dclips, bias, clips = call(

time: 27.7 us -> 27.7 us (level)
  waiting for transfers between devices: 7.28 us -> 4.98 us
  starting transfers between devices: 9.75 us -> 12 us
    ppermute x2 -> x1, waiting for transfers between devices: 2.3 us -> 0.01 us  [shift(): lax.ppermute(array, 'seq', [(r, (r + d) % seq_count) for r in range(seq_c...]
    ppermute x0 -> x1, starting transfers between devices: none -> 1.92 us  [shift_up(): lax.ppermute(array, 'seq', [(r, r + d) for r in range(seq_count - d)])]
    ppermute x1, starting transfers between devices: 1.74 us -> 2.15 us  [unshift(): lax.ppermute(array, 'seq', [((r + d) % seq_count, r) for r in range(seq_c...]
    ppermute x2 -> x1, starting transfers between devices: 3.11 us -> 3.03 us  [shift(): lax.ppermute(array, 'seq', [(r, (r + d) % seq_count) for r in range(seq_c...]
  transfers between devices with their start and end apart: 4 -> 4, of which waited for: 4 -> 2; matrix products, arithmetic and copies ran while one was open for 0% -> 0% of each run, Pallas kernels for 23% -> 23%
where the time goes in v3:
time: 27.7 us; the launch traced here: 27.5 us
  starting transfers between devices  12 us (43%)
  Pallas kernels  9.8 us (35%)
  waiting for transfers between devices  4.98 us (18%)
  between operations  0.69 us (2%)
    pallas_call x5, Pallas kernels, call(): pl.pallas_call(kernel, out_shape=outs, in_specs=in_specs or [vmem] * len(...  9.8 us
    all_to_all x1, starting transfers between devices, on_device(): lax.all_to_all(spread, ('dp', 'seq'), split_axis=0, concat_axis=0, axis_i...  4.89 us
    all_to_all x1, waiting for transfers between devices, on_device(): lax.all_to_all(spread, ('dp', 'seq'), split_axis=0, concat_axis=0, axis_i...  4.23 us
    ppermute x1, starting transfers between devices, shift(): lax.ppermute(array, 'seq', [(r, (r + d) % seq_count) for r in range(seq_c...  3.03 us
    ppermute x1, starting transfers between devices, unshift(): lax.ppermute(array, 'seq', [((r + d) % seq_count, r) for r in range(seq_c...  2.15 us
    ppermute x1, starting transfers between devices, shift_up(): lax.ppermute(array, 'seq', [(r, r + d) for r in range(seq_count - d)])  1.92 us
    ppermute x1, waiting for transfers between devices, unshift(): lax.ppermute(array, 'seq', [((r + d) % seq_count, r) for r in range(seq_c...  0.74 us
  transfers between devices with their start and end apart: 4, of which 2 were waited for; matrix products, arithmetic and copies ran while one was open for 0% of the time, Pallas kernels for 23%

profile of v3, /device:TPU:0, one launch (start us, length us, event | category | flops | bytes accessed | tf_op | source)
XLA Modules:
  0.0 27.5 jit_solution(9450126343276890990)
XLA Ops:
  0.6 3.0 %collective-permute-start = (bf16[128,512]{1,0:T(8,128)(2,1)}, bf16[128,512]{1,0:T(8,128)(2,1)S(1)}, u32[]{:S(2)}, u32[]{:S(2)}) collective-permute-start(bf16[128,512]{1,0:T(8,128)(2,1)} %key_hbm.1), channel_id=1, source_target_pairs={{0,1},{1,0},{2,3},{3,2},{4,5},{5,4},{6,7},{7,6},{8,9},{9,8},{10,11... | collective-permute-start | bytes 393224 | tf_op jit(solution)/shard_map/ppermute | solution.py:310
  3.7 1.9 %collective-permute-start.1 = (bf16[128,512]{1,0:T(8,128)(2,1)}, bf16[128,512]{1,0:T(8,128)(2,1)S(1)}, u32[]{:S(2)}, u32[]{:S(2)}) collective-permute-start(bf16[128,512]{1,0:T(8,128)(2,1)} %value_hbm.1), channel_id=1, source_target_pairs={{0,1},{2,3},{4,5},{6,7},{8,9},{10,11},{12,13},{14,15},{16,17},{18,... | collective-permute-start | bytes 393224 | tf_op jit(solution)/shard_map/ppermute | solution.py:316
  5.6 2.6 %prep.1 = (bf16[512,1024]{1,0:T(8,128)(2,1)S(1)}, bf16[512,1024]{1,0:T(8,128)(2,1)S(1)}, bf16[128,1024]{1,0:T(8,128)(2,1)S(1)}, f32[128,1024]{1,0:T(8,128)}, f32...) custom-call(bf16[128,4096]{1,0:T(8,128)(2,1)} %q_hbm.1, bf16[128,4096]{1,0:T(8,128)(2,1)} %g_hbm.1, ...), custom_call_target="tpu_custom_call" | custom-call | flops 134217728 | bytes 1048576 | tf_op jit(solution)/shard_map/prep/pallas_call | solution.py:298
  8.2 0.0 collective-permute-done.rest_0_
  8.2 1.5 %score.1 = (bf16[128,4096]{1,0:T(8,128)(2,1)S(1)}, bf16[256,512]{1,0:T(8,128)(2,1)S(1)}, f32[128,512]{1,0:T(8,128)S(1)}) custom-call(bf16[512,1024]{1,0:T(8,128)(2,1)S(1)} %get-tuple-element.24.qt_ref, bf16[128,1024]{1,0:T(8,128)(2,1)S(1)} %get-tuple-element.25.quant_ref, f32[128,128]{1,0:T(8,128)S(1)} %get-tuple-element.26.bias_ref, ...), custom_call_target="tpu_custom_call" | custom-call | flops 268435456 | bytes 1048576 | tf_op jit(solution)/shard_map/score/pallas_call | solution.py:298
  9.8 0.0 collective-permute-done.1.rest_0_
  9.8 2.9 %grad.1 = (bf16[128,4096]{1,0:T(8,128)(2,1)S(1)}, bf16[256,512]{1,0:T(8,128)(2,1)S(1)}, bf16[128,1024]{1,0:T(8,128)(2,1)S(1)}, bf16[128,1024]{1,0:T(8,128)(2,1)S(1)}, bf16[32,8,128]{2,1,0:T(8,128)(2,1)}) custom-call(bf16[512,1024]{1,0:T(8,128)(2,1)S(1)} %get-tuple-element.24.qt_ref, bf16[512,1024]{1,0:T(8,128)(2,1)S(1)} %get-tuple-element.29.gt_ref, ...), custom_call_target="tpu_custom_call" | custom-call | flops 805306368 | bytes 1048576 | tf_op jit(solution)/shard_map/grad/pallas_call | solution.py:298
  12.7 2.1 %collective-permute-start.2 = (bf16[128,1024]{1,0:T(8,128)(2,1)S(1)}, bf16[128,1024]{1,0:T(8,128)(2,1)S(1)}, u32[]{:S(2)}, u32[]{:S(2)}) collective-permute-start(bf16[128,1024]{1,0:T(8,128)(2,1)S(1)} %get-tuple-element.37), channel_id=1, source_target_pairs={{1,0},{0,1},{3,2},{2,3},{5,4},{4,5},{7,6},{6,7},{9,8},{8,9},{11,10... | collective-permute-start | bytes 786440 | tf_op jit(solution)/shard_map/ppermute | solution.py:313
  14.8 4.9 %all-to-all-start = ((bf16[32,8,128]{2,1,0:T(8,128)(2,1)}), bf16[32,8,128]{2,1,0:T(8,128)(2,1)S(1)}, u32[]{:S(2)}, u32[]{:S(2)}) async-start(bf16[32,8,128]{2,1,0:T(8,128)(2,1)} %get-tuple-element.42), calls=%async_computation | async-start | bytes 131072 | tf_op jit(solution)/shard_map/all_to_all | solution.py:377
  19.7 0.7 %collective-permute-done.2.rest_0_ = bf16[128,1024]{1,0:T(8,128)(2,1)S(1)} collective-permute-done((bf16[128,1024]{1,0:T(8,128)(2,1)S(1)}, bf16[128,1024]{1,0:T(8,128)(2,1)S(1)}, u32[]{:S(2)}, u32[]{:S(2)}) %collective-permute-start.2) | collective-permute-done | bytes 262176 | tf_op jit(solution)/shard_map/ppermute | solution.py:313
  20.5 2.1 %output.1 = (bf16[128,4096]{1,0:T(8,128)(2,1)}, bf16[128,4096]{1,0:T(8,128)(2,1)}, bf16[128,512]{1,0:T(8,128)(2,1)}, bf16[128,512]{1,0:T(8,128)(2,1)}) custom-call(bf16[128,4096]{1,0:T(8,128)(2,1)S(1)} %get-tuple-element.28.p_ref, bf16[128,4096]{1,0:T(8,128)(2,1)S(1)} %get-tuple-element.32.ds_ref, bf16[256,512]{1,0:T(8,128)(2,1)S(1)} %get-tuple-element.33.k2_ref, ...), custom_call_target="tpu_custom_call" | custom-call | flops 536870912 | bytes 1048576 | tf_op jit(solution)/shard_map/output/pallas_call | solution.py:298
  22.6 4.2 %all-to-all-done.parts_ref = bf16[32,8,128]{2,1,0:T(8,128)(2,1)S(1)} async-done(((bf16[32,8,128]{2,1,0:T(8,128)(2,1)}), bf16[32,8,128]{2,1,0:T(8,128)(2,1)S(1)}, u32[]{:S(2)}, u32[]{:S(2)}) %all-to-all-start) | async-done | bytes 65568 | tf_op jit(solution)/shard_map/all_to_all | solution.py:377
  26.9 0.6 %total.1 = f32[8,128]{1,0:T(8,128)} custom-call(bf16[32,8,128]{2,1,0:T(8,128)(2,1)S(1)} %all-to-all-done.parts_ref, bf16[128,512]{1,0:T(8,128)(2,1)} %get-tuple-element.21.after_ref), custom_call_target="tpu_custom_call" | custom-call | flops 32768 | bytes 1048576 | tf_op jit(solution)/shard_map/total/pallas_call | solution.py:298
Async XLA Ops:
  0.6 7.6 %collective-permute-start = (bf16[128,512]{1,0:T(8,128)(2,1)}, bf16[128,512]{1,0:T(8,128)(2,1)S(1)}, u32[]{:S(2)}, u32[]{:S(2)}) collective-permute-start(bf16[128,512]{1,0:T(8,128)(2,1)} %key_hbm.1), channel_id=1, source_target_pairs={{0,1},{1,0},{2,3},{3,2},{4,5},{5,4},{6,7},{7,6},{8,9},{9,8},{10,11... | collective-permute-start | bytes 393224 | tf_op jit(solution)/shard_map/ppermute | solution.py:310
  3.7 6.1 %collective-permute-start.1 = (bf16[128,512]{1,0:T(8,128)(2,1)}, bf16[128,512]{1,0:T(8,128)(2,1)S(1)}, u32[]{:S(2)}, u32[]{:S(2)}) collective-permute-start(bf16[128,512]{1,0:T(8,128)(2,1)} %value_hbm.1), channel_id=1, source_target_pairs={{0,1},{2,3},{4,5},{6,7},{8,9},{10,11},{12,13},{14,15},{16,17},{18,... | collective-permute-start | bytes 393224 | tf_op jit(solution)/shard_map/ppermute | solution.py:316
  12.7 7.8 %collective-permute-start.2 = (bf16[128,1024]{1,0:T(8,128)(2,1)S(1)}, bf16[128,1024]{1,0:T(8,128)(2,1)S(1)}, u32[]{:S(2)}, u32[]{:S(2)}) collective-permute-start(bf16[128,1024]{1,0:T(8,128)(2,1)S(1)} %get-tuple-element.37), channel_id=1, source_target_pairs={{1,0},{0,1},{3,2},{2,3},{5,4},{4,5},{7,6},{6,7},{9,8},{8,9},{11,10... | collective-permute-start | bytes 786440 | tf_op jit(solution)/shard_map/ppermute | solution.py:313
  14.8 12.0 %all-to-all-start = ((bf16[32,8,128]{2,1,0:T(8,128)(2,1)}), bf16[32,8,128]{2,1,0:T(8,128)(2,1)S(1)}, u32[]{:S(2)}, u32[]{:S(2)}) async-start(bf16[32,8,128]{2,1,0:T(8,128)(2,1)} %get-tuple-element.42), calls=%async_computation | async-start | bytes 131072 | tf_op jit(solution)/shard_map/all_to_all | solution.py:377

commit v4 on v0

--- a/solution.py
+++ b/solution.py
@@ -107,9 +107,10 @@
     return jnp.concatenate([first, x[2 * rows:]], axis=0) if nb > 1 else first
 
 
-def split(near_b, far_b, x, nb):
+def split(near_b, x, nb):
     rows = near_b.shape[0]
-    parts = [x[:rows] * near_b, x[:rows] * far_b]
+    own = x[:rows] * near_b
+    parts = [own, x[:rows] - own]
     if nb > 1:
         parts.append(x[rows:])
     return jnp.concatenate(parts, axis=0)
@@ -154,7 +155,6 @@
     scale = hd ** -0.5
     near = near_mask(rows)
     near_b = near.astype(F32).astype(BF16)
-    far_b = 1.0 - near_b
 
     def k_cols(n):
         return slice(n * hd, (n + 1) * hd)
@@ -164,7 +164,7 @@
 
     def value_side(n):
         p2 = jnp.concatenate(
-            [split(near_b, far_b, p_ref[:, n * span + h * rows:n * span + (h + 1) * rows], nb) for h in range(heads)],
+            [split(near_b, p_ref[:, n * span + h * rows:n * span + (h + 1) * rows], nb) for h in range(heads)],
             axis=1,
         )
         v_grad = lax.dot_general(gt_ref[k_cols(n), :], p2, ACROSS, preferred_element_type=F32).T
@@ -191,7 +191,7 @@
             delta = jnp.sum(p * dp, axis=0, keepdims=True)
             ds_b = (p * (dp - delta)).astype(BF16)
             ds_ref[:, at] = ds_b
-            ds.append(split(near_b, far_b, ds_b, nb))
+            ds.append(split(near_b, ds_b, nb))
         return jnp.concatenate(ds, axis=1)
 
     def key_side(n, ds2):
@@ -231,7 +231,6 @@
     hd = k2_ref.shape[1] // kv_heads
     heads = group // hd
     near_b = near_mask(rows).astype(F32).astype(BF16)
-    far_b = 1.0 - near_b
 
     def copies(n):
         cols = pl.ds(pl.multiple_of(n * group, group), group)
@@ -246,7 +245,7 @@
             at = pl.ds(pl.multiple_of(n * heads * rows, rows), heads * rows)
             x = right[:, at]
             x2 = jnp.concatenate(
-                [split(near_b, far_b, x[:, h * rows:(h + 1) * rows], nb) for h in range(heads)], axis=1
+                [split(near_b, x[:, h * rows:(h + 1) * rows], nb) for h in range(heads)], axis=1
             )
             y = jnp.dot(left[:, cols].T, x2, preferred_element_type=F32)
             y = (y if scale is None else y * scale).astype(BF16)

time: 27.7 us -> 27.7 us (level)
  no operation moved by 1% of the time
where the time goes in v4:
time: 27.7 us; the launch traced here: 27.5 us
  Pallas kernels  9.95 us (36%)
  starting transfers between devices  9.74 us (35%)
  waiting for transfers between devices  7.14 us (26%)
  between operations  0.67 us (2%)
    pallas_call x5, Pallas kernels, call(): pl.pallas_call(kernel, out_shape=outs, in_specs=in_specs or [vmem] * len(...  9.95 us
    all_to_all x1, starting transfers between devices, on_device(): lax.all_to_all(spread, ('dp', 'seq'), split_axis=0, concat_axis=0, axis_i...  4.89 us
    all_to_all x1, waiting for transfers between devices, on_device(): lax.all_to_all(spread, ('dp', 'seq'), split_axis=0, concat_axis=0, axis_i...  3.99 us
    ppermute x2, starting transfers between devices, shift(): lax.ppermute(array, 'seq', [(r, (r + d) % seq_count) for r in range(seq_c...  3.11 us
    ppermute x2, waiting for transfers between devices, shift(): lax.ppermute(array, 'seq', [(r, (r + d) % seq_count) for r in range(seq_c...  2.3 us
    ppermute x1, starting transfers between devices, unshift(): lax.ppermute(array, 'seq', [((r + d) % seq_count, r) for r in range(seq_c...  1.74 us
    ppermute x1, waiting for transfers between devices, unshift(): lax.ppermute(array, 'seq', [((r + d) % seq_count, r) for r in range(seq_c...  0.85 us
  transfers between devices with their start and end apart: 4, of which 4 were waited for; matrix products, arithmetic and copies ran while one was open for 0% of the time, Pallas kernels for 23%

profile of v4, /device:TPU:0, one launch (start us, length us, event | category | flops | bytes accessed | tf_op | source)
XLA Modules:
  0.0 27.5 jit_solution(12235552852342962914)
XLA Ops:
  0.6 3.0 %collective-permute-start = (bf16[128,512]{1,0:T(8,128)(2,1)}, bf16[128,512]{1,0:T(8,128)(2,1)S(1)}, u32[]{:S(2)}, u32[]{:S(2)}) collective-permute-start(bf16[128,512]{1,0:T(8,128)(2,1)} %key_hbm.1), channel_id=1, source_target_pairs={{0,1},{1,0},{2,3},{3,2},{4,5},{5,4},{6,7},{7,6},{8,9},{9,8},{10,11... | collective-permute-start | bytes 393224 | tf_op jit(solution)/shard_map/ppermute | solution.py:309
  3.7 0.1 collective-permute-start.1
  3.7 2.6 %prep.1 = (bf16[512,1024]{1,0:T(8,128)(2,1)S(1)}, bf16[512,1024]{1,0:T(8,128)(2,1)S(1)}, bf16[128,1024]{1,0:T(8,128)(2,1)S(1)}, f32[128,1024]{1,0:T(8,128)}, f32...) custom-call(bf16[128,4096]{1,0:T(8,128)(2,1)} %q_hbm.1, bf16[128,4096]{1,0:T(8,128)(2,1)} %g_hbm.1, ...), custom_call_target="tpu_custom_call" | custom-call | flops 134217728 | bytes 1048576 | tf_op jit(solution)/shard_map/prep/pallas_call | solution.py:297
  6.3 1.9 %collective-permute-done.rest_0_ = bf16[128,512]{1,0:T(8,128)(2,1)S(1)} collective-permute-done((bf16[128,512]{1,0:T(8,128)(2,1)}, bf16[128,512]{1,0:T(8,128)(2,1)S(1)}, u32[]{:S(2)}, u32[]{:S(2)}) %collective-permute-start) | collective-permute-done | bytes 131104 | tf_op jit(solution)/shard_map/ppermute | solution.py:309
  8.2 1.5 %score.1 = (bf16[128,4096]{1,0:T(8,128)(2,1)S(1)}, bf16[256,512]{1,0:T(8,128)(2,1)S(1)}, f32[128,512]{1,0:T(8,128)S(1)}) custom-call(bf16[512,1024]{1,0:T(8,128)(2,1)S(1)} %get-tuple-element.24.qt_ref, bf16[128,1024]{1,0:T(8,128)(2,1)S(1)} %get-tuple-element.25.quant_ref, f32[128,128]{1,0:T(8,128)S(1)} %get-tuple-element.26.bias_ref, ...), custom_call_target="tpu_custom_call" | custom-call | flops 268435456 | bytes 1048576 | tf_op jit(solution)/shard_map/score/pallas_call | solution.py:297
  9.7 0.4 %collective-permute-done.1.rest_0_ = bf16[128,512]{1,0:T(8,128)(2,1)S(1)} collective-permute-done((bf16[128,512]{1,0:T(8,128)(2,1)}, bf16[128,512]{1,0:T(8,128)(2,1)S(1)}, u32[]{:S(2)}, u32[]{:S(2)}) %collective-permute-start.1) | collective-permute-done | bytes 131104 | tf_op jit(solution)/shard_map/ppermute | solution.py:309
  10.2 2.9 %grad.1 = (bf16[128,4096]{1,0:T(8,128)(2,1)S(1)}, bf16[256,512]{1,0:T(8,128)(2,1)S(1)}, bf16[128,1024]{1,0:T(8,128)(2,1)S(1)}, bf16[128,1024]{1,0:T(8,128)(2,1)S(1)}, bf16[32,8,128]{2,1,0:T(8,128)(2,1)}) custom-call(bf16[512,1024]{1,0:T(8,128)(2,1)S(1)} %get-tuple-element.24.qt_ref, bf16[512,1024]{1,0:T(8,128)(2,1)S(1)} %get-tuple-element.29.gt_ref, ...), custom_call_target="tpu_custom_call" | custom-call | flops 805306368 | bytes 1048576 | tf_op jit(solution)/shard_map/grad/pallas_call | solution.py:297
  13.1 1.7 %collective-permute-start.2 = (bf16[128,1024]{1,0:T(8,128)(2,1)S(1)}, bf16[128,1024]{1,0:T(8,128)(2,1)S(1)}, u32[]{:S(2)}, u32[]{:S(2)}) collective-permute-start(bf16[128,1024]{1,0:T(8,128)(2,1)S(1)} %get-tuple-element.37), channel_id=1, source_target_pairs={{1,0},{0,1},{3,2},{2,3},{5,4},{4,5},{7,6},{6,7},{9,8},{8,9},{11,10... | collective-permute-start | bytes 786440 | tf_op jit(solution)/shard_map/ppermute | solution.py:312
  14.8 4.9 %all-to-all-start = ((bf16[32,8,128]{2,1,0:T(8,128)(2,1)}), bf16[32,8,128]{2,1,0:T(8,128)(2,1)S(1)}, u32[]{:S(2)}, u32[]{:S(2)}) async-start(bf16[32,8,128]{2,1,0:T(8,128)(2,1)} %get-tuple-element.42), calls=%async_computation | async-start | bytes 131072 | tf_op jit(solution)/shard_map/all_to_all | solution.py:373
  19.8 0.9 %collective-permute-done.2.rest_0_ = bf16[128,1024]{1,0:T(8,128)(2,1)S(1)} collective-permute-done((bf16[128,1024]{1,0:T(8,128)(2,1)S(1)}, bf16[128,1024]{1,0:T(8,128)(2,1)S(1)}, u32[]{:S(2)}, u32[]{:S(2)}) %collective-permute-start.2) | collective-permute-done | bytes 262176 | tf_op jit(solution)/shard_map/ppermute | solution.py:312
  20.6 2.3 %output.1 = (bf16[128,4096]{1,0:T(8,128)(2,1)}, bf16[128,4096]{1,0:T(8,128)(2,1)}, bf16[128,512]{1,0:T(8,128)(2,1)}, bf16[128,512]{1,0:T(8,128)(2,1)}) custom-call(bf16[128,4096]{1,0:T(8,128)(2,1)S(1)} %get-tuple-element.28.p_ref, bf16[128,4096]{1,0:T(8,128)(2,1)S(1)} %get-tuple-element.32.ds_ref, bf16[256,512]{1,0:T(8,128)(2,1)S(1)} %get-tuple-element.33.k2_ref, ...), custom_call_target="tpu_custom_call" | custom-call | flops 536870912 | bytes 1048576 | tf_op jit(solution)/shard_map/output/pallas_call | solution.py:297
  22.9 4.0 %all-to-all-done.parts_ref = bf16[32,8,128]{2,1,0:T(8,128)(2,1)S(1)} async-done(((bf16[32,8,128]{2,1,0:T(8,128)(2,1)}), bf16[32,8,128]{2,1,0:T(8,128)(2,1)S(1)}, u32[]{:S(2)}, u32[]{:S(2)}) %all-to-all-start) | async-done | bytes 65568 | tf_op jit(solution)/shard_map/all_to_all | solution.py:373
  26.9 0.6 %total.1 = f32[8,128]{1,0:T(8,128)} custom-call(bf16[32,8,128]{2,1,0:T(8,128)(2,1)S(1)} %all-to-all-done.parts_ref, bf16[128,512]{1,0:T(8,128)(2,1)} %get-tuple-element.21.after_ref), custom_call_target="tpu_custom_call" | custom-call | flops 32768 | bytes 1048576 | tf_op jit(solution)/shard_map/total/pallas_call | solution.py:297
Async XLA Ops:
  0.6 7.6 %collective-permute-start = (bf16[128,512]{1,0:T(8,128)(2,1)}, bf16[128,512]{1,0:T(8,128)(2,1)S(1)}, u32[]{:S(2)}, u32[]{:S(2)}) collective-permute-start(bf16[128,512]{1,0:T(8,128)(2,1)} %key_hbm.1), channel_id=1, source_target_pairs={{0,1},{1,0},{2,3},{3,2},{4,5},{5,4},{6,7},{7,6},{8,9},{9,8},{10,11... | collective-permute-start | bytes 393224 | tf_op jit(solution)/shard_map/ppermute | solution.py:309
  3.7 6.5 %collective-permute-start.1 = (bf16[128,512]{1,0:T(8,128)(2,1)}, bf16[128,512]{1,0:T(8,128)(2,1)S(1)}, u32[]{:S(2)}, u32[]{:S(2)}) collective-permute-start(bf16[128,512]{1,0:T(8,128)(2,1)} %value_hbm.1), channel_id=1, source_target_pairs={{0,1},{1,0},{2,3},{3,2},{4,5},{5,4},{6,7},{7,6},{8,9},{9,8},{10,11... | collective-permute-start | bytes 393224 | tf_op jit(solution)/shard_map/ppermute | solution.py:309
  13.1 7.5 %collective-permute-start.2 = (bf16[128,1024]{1,0:T(8,128)(2,1)S(1)}, bf16[128,1024]{1,0:T(8,128)(2,1)S(1)}, u32[]{:S(2)}, u32[]{:S(2)}) collective-permute-start(bf16[128,1024]{1,0:T(8,128)(2,1)S(1)} %get-tuple-element.37), channel_id=1, source_target_pairs={{1,0},{0,1},{3,2},{2,3},{5,4},{4,5},{7,6},{6,7},{9,8},{8,9},{11,10... | collective-permute-start | bytes 786440 | tf_op jit(solution)/shard_map/ppermute | solution.py:312
  14.8 12.0 %all-to-all-start = ((bf16[32,8,128]{2,1,0:T(8,128)(2,1)}), bf16[32,8,128]{2,1,0:T(8,128)(2,1)S(1)}, u32[]{:S(2)}, u32[]{:S(2)}) async-start(bf16[32,8,128]{2,1,0:T(8,128)(2,1)} %get-tuple-element.42), calls=%async_computation | async-start | bytes 131072 | tf_op jit(solution)/shard_map/all_to_all | solution.py:373

commit v5 on v0

--- a/solution.py
+++ b/solution.py
@@ -162,25 +162,30 @@
     def v_cols(n):
         return slice(width + n * hd, width + (n + 1) * hd)
 
+    vdclips = {}
+
     def value_side(n):
+        vs, vd = [quant_ref[:, v_cols(n)]], [dclip_ref[:, v_cols(n)]]
+        for d in far_order(nb):
+            q, _, dc = quant_parts(far_v[d - 1][:, k_cols(n)].astype(F32), clip_ref[1, n:n + 1, :])
+            vs.append(q.astype(BF16))
+            vd.append(dc)
+        vdclips[n] = vd
+        v2 = jnp.concatenate(vs, axis=0)
+        v2_ref[:, k_cols(n)] = v2
+        return jnp.dot(v2, gt_ref[k_cols(n), :], preferred_element_type=F32)
+
+    def value_grad(n):
         p2 = jnp.concatenate(
             [split(near_b, far_b, p_ref[:, n * span + h * rows:n * span + (h + 1) * rows], nb) for h in range(heads)],
             axis=1,
         )
         v_grad = lax.dot_general(gt_ref[k_cols(n), :], p2, ACROSS, preferred_element_type=F32).T
-        vs, vd = [quant_ref[:, v_cols(n)]], [dclip_ref[:, v_cols(n)]]
-        for d in far_order(nb):
-            q, _, dc = quant_parts(far_v[d - 1][:, k_cols(n)].astype(F32), clip_ref[1, n:n + 1, :])
-            vs.append(q.astype(BF16))
-            vd.append(dc)
-        v2 = jnp.concatenate(vs, axis=0)
-        v2_ref[:, k_cols(n)] = v2
         grad_ref[:, v_cols(n)] = v_grad[:rows].astype(BF16)
         far_ref[:, v_cols(n)] = v_grad[rows:].astype(BF16)
         scale_ref[kv_heads + n:kv_heads + n + 1, :] = jnp.sum(
-            v_grad * jnp.concatenate(vd, axis=0), axis=0, keepdims=True
+            v_grad * jnp.concatenate(vdclips[n], axis=0), axis=0, keepdims=True
         )
-        return jnp.dot(v2, gt_ref[k_cols(n), :], preferred_element_type=F32)
 
     def score_side(n, d_all):
         ds = []
@@ -205,6 +210,7 @@
     ahead, behind = value_side(0), None
     for n in range(kv_heads):
         d_all, ahead = ahead, value_side(n + 1) if n + 1 < kv_heads else None
+        value_grad(n)
         ds2 = score_side(n, d_all)
         if behind is not None:
             key_side(n - 1, behind)

time: 27.7 us -> 27.8 us (level)
  no operation moved by 1% of the time
where the time goes in v5:
time: 27.8 us; the launch traced here: 27.6 us
  Pallas kernels  9.86 us (35%)
  starting transfers between devices  9.74 us (35%)
  waiting for transfers between devices  7.28 us (26%)
  between operations  0.67 us (2%)
    pallas_call x5, Pallas kernels, call(): pl.pallas_call(kernel, out_shape=outs, in_specs=in_specs or [vmem] * len(...  9.86 us
    all_to_all x1, starting transfers between devices, on_device(): lax.all_to_all(spread, ('dp', 'seq'), split_axis=0, concat_axis=0, axis_i...  4.89 us
    all_to_all x1, waiting for transfers between devices, on_device(): lax.all_to_all(spread, ('dp', 'seq'), split_axis=0, concat_axis=0, axis_i...  4.13 us
    ppermute x2, starting transfers between devices, shift(): lax.ppermute(array, 'seq', [(r, (r + d) % seq_count) for r in range(seq_c...  3.11 us
    ppermute x2, waiting for transfers between devices, shift(): lax.ppermute(array, 'seq', [(r, (r + d) % seq_count) for r in range(seq_c...  2.3 us
    ppermute x1, starting transfers between devices, unshift(): lax.ppermute(array, 'seq', [((r + d) % seq_count, r) for r in range(seq_c...  1.74 us
    ppermute x1, waiting for transfers between devices, unshift(): lax.ppermute(array, 'seq', [((r + d) % seq_count, r) for r in range(seq_c...  0.85 us
  transfers between devices with their start and end apart: 4, of which 4 were waited for; matrix products, arithmetic and copies ran while one was open for 0% of the time, Pallas kernels for 23%

profile of v5, /device:TPU:0, one launch (start us, length us, event | category | flops | bytes accessed | tf_op | source)
XLA Modules:
  0.0 27.6 jit_solution(4007555374974740744)
XLA Ops:
  0.6 3.0 %collective-permute-start = (bf16[128,512]{1,0:T(8,128)(2,1)}, bf16[128,512]{1,0:T(8,128)(2,1)S(1)}, u32[]{:S(2)}, u32[]{:S(2)}) collective-permute-start(bf16[128,512]{1,0:T(8,128)(2,1)} %key_hbm.1), channel_id=1, source_target_pairs={{0,1},{1,0},{2,3},{3,2},{4,5},{5,4},{6,7},{7,6},{8,9},{9,8},{10,11... | collective-permute-start | bytes 393224 | tf_op jit(solution)/shard_map/ppermute | solution.py:316
  3.7 0.1 collective-permute-start.1
  3.7 2.6 %prep.1 = (bf16[512,1024]{1,0:T(8,128)(2,1)S(1)}, bf16[512,1024]{1,0:T(8,128)(2,1)S(1)}, bf16[128,1024]{1,0:T(8,128)(2,1)S(1)}, f32[128,1024]{1,0:T(8,128)}, f32...) custom-call(bf16[128,4096]{1,0:T(8,128)(2,1)} %q_hbm.1, bf16[128,4096]{1,0:T(8,128)(2,1)} %g_hbm.1, ...), custom_call_target="tpu_custom_call" | custom-call | flops 134217728 | bytes 1048576 | tf_op jit(solution)/shard_map/prep/pallas_call | solution.py:304
  6.3 1.9 %collective-permute-done.rest_0_ = bf16[128,512]{1,0:T(8,128)(2,1)S(1)} collective-permute-done((bf16[128,512]{1,0:T(8,128)(2,1)}, bf16[128,512]{1,0:T(8,128)(2,1)S(1)}, u32[]{:S(2)}, u32[]{:S(2)}) %collective-permute-start) | collective-permute-done | bytes 131104 | tf_op jit(solution)/shard_map/ppermute | solution.py:316
  8.2 1.5 %score.1 = (bf16[128,4096]{1,0:T(8,128)(2,1)S(1)}, bf16[256,512]{1,0:T(8,128)(2,1)S(1)}, f32[128,512]{1,0:T(8,128)S(1)}) custom-call(bf16[512,1024]{1,0:T(8,128)(2,1)S(1)} %get-tuple-element.24.qt_ref, bf16[128,1024]{1,0:T(8,128)(2,1)S(1)} %get-tuple-element.25.quant_ref, f32[128,128]{1,0:T(8,128)S(1)} %get-tuple-element.26.bias_ref, ...), custom_call_target="tpu_custom_call" | custom-call | flops 268435456 | bytes 1048576 | tf_op jit(solution)/shard_map/score/pallas_call | solution.py:304
  9.7 0.4 %collective-permute-done.1.rest_0_ = bf16[128,512]{1,0:T(8,128)(2,1)S(1)} collective-permute-done((bf16[128,512]{1,0:T(8,128)(2,1)}, bf16[128,512]{1,0:T(8,128)(2,1)S(1)}, u32[]{:S(2)}, u32[]{:S(2)}) %collective-permute-start.1) | collective-permute-done | bytes 131104 | tf_op jit(solution)/shard_map/ppermute | solution.py:316
  10.2 3.0 %grad.1 = (bf16[128,4096]{1,0:T(8,128)(2,1)S(1)}, bf16[256,512]{1,0:T(8,128)(2,1)S(1)}, bf16[128,1024]{1,0:T(8,128)(2,1)S(1)}, bf16[128,1024]{1,0:T(8,128)(2,1)S(1)}, bf16[32,8,128]{2,1,0:T(8,128)(2,1)}) custom-call(bf16[512,1024]{1,0:T(8,128)(2,1)S(1)} %get-tuple-element.24.qt_ref, bf16[512,1024]{1,0:T(8,128)(2,1)S(1)} %get-tuple-element.29.gt_ref, ...), custom_call_target="tpu_custom_call" | custom-call | flops 805306368 | bytes 1048576 | tf_op jit(solution)/shard_map/grad/pallas_call | solution.py:304
  13.2 1.7 %collective-permute-start.2 = (bf16[128,1024]{1,0:T(8,128)(2,1)S(1)}, bf16[128,1024]{1,0:T(8,128)(2,1)S(1)}, u32[]{:S(2)}, u32[]{:S(2)}) collective-permute-start(bf16[128,1024]{1,0:T(8,128)(2,1)S(1)} %get-tuple-element.37), channel_id=1, source_target_pairs={{1,0},{0,1},{3,2},{2,3},{5,4},{4,5},{7,6},{6,7},{9,8},{8,9},{11,10... | collective-permute-start | bytes 786440 | tf_op jit(solution)/shard_map/ppermute | solution.py:319
  14.9 4.9 %all-to-all-start = ((bf16[32,8,128]{2,1,0:T(8,128)(2,1)}), bf16[32,8,128]{2,1,0:T(8,128)(2,1)S(1)}, u32[]{:S(2)}, u32[]{:S(2)}) async-start(bf16[32,8,128]{2,1,0:T(8,128)(2,1)} %get-tuple-element.42), calls=%async_computation | async-start | bytes 131072 | tf_op jit(solution)/shard_map/all_to_all | solution.py:380
  19.8 0.8 %collective-permute-done.2.rest_0_ = bf16[128,1024]{1,0:T(8,128)(2,1)S(1)} collective-permute-done((bf16[128,1024]{1,0:T(8,128)(2,1)S(1)}, bf16[128,1024]{1,0:T(8,128)(2,1)S(1)}, u32[]{:S(2)}, u32[]{:S(2)}) %collective-permute-start.2) | collective-permute-done | bytes 262176 | tf_op jit(solution)/shard_map/ppermute | solution.py:319
  20.7 2.1 %output.1 = (bf16[128,4096]{1,0:T(8,128)(2,1)}, bf16[128,4096]{1,0:T(8,128)(2,1)}, bf16[128,512]{1,0:T(8,128)(2,1)}, bf16[128,512]{1,0:T(8,128)(2,1)}) custom-call(bf16[128,4096]{1,0:T(8,128)(2,1)S(1)} %get-tuple-element.28.p_ref, bf16[128,4096]{1,0:T(8,128)(2,1)S(1)} %get-tuple-element.32.ds_ref, bf16[256,512]{1,0:T(8,128)(2,1)S(1)} %get-tuple-element.33.k2_ref, ...), custom_call_target="tpu_custom_call" | custom-call | flops 536870912 | bytes 1048576 | tf_op jit(solution)/shard_map/output/pallas_call | solution.py:304
  22.8 4.1 %all-to-all-done.parts_ref = bf16[32,8,128]{2,1,0:T(8,128)(2,1)S(1)} async-done(((bf16[32,8,128]{2,1,0:T(8,128)(2,1)}), bf16[32,8,128]{2,1,0:T(8,128)(2,1)S(1)}, u32[]{:S(2)}, u32[]{:S(2)}) %all-to-all-start) | async-done | bytes 65568 | tf_op jit(solution)/shard_map/all_to_all | solution.py:380
  26.9 0.6 %total.1 = f32[8,128]{1,0:T(8,128)} custom-call(bf16[32,8,128]{2,1,0:T(8,128)(2,1)S(1)} %all-to-all-done.parts_ref, bf16[128,512]{1,0:T(8,128)(2,1)} %get-tuple-element.21.after_ref), custom_call_target="tpu_custom_call" | custom-call | flops 32768 | bytes 1048576 | tf_op jit(solution)/shard_map/total/pallas_call | solution.py:304
Async XLA Ops:
  0.6 7.6 %collective-permute-start = (bf16[128,512]{1,0:T(8,128)(2,1)}, bf16[128,512]{1,0:T(8,128)(2,1)S(1)}, u32[]{:S(2)}, u32[]{:S(2)}) collective-permute-start(bf16[128,512]{1,0:T(8,128)(2,1)} %key_hbm.1), channel_id=1, source_target_pairs={{0,1},{1,0},{2,3},{3,2},{4,5},{5,4},{6,7},{7,6},{8,9},{9,8},{10,11... | collective-permute-start | bytes 393224 | tf_op jit(solution)/shard_map/ppermute | solution.py:316
  3.7 6.5 %collective-permute-start.1 = (bf16[128,512]{1,0:T(8,128)(2,1)}, bf16[128,512]{1,0:T(8,128)(2,1)S(1)}, u32[]{:S(2)}, u32[]{:S(2)}) collective-permute-start(bf16[128,512]{1,0:T(8,128)(2,1)} %value_hbm.1), channel_id=1, source_target_pairs={{0,1},{1,0},{2,3},{3,2},{4,5},{5,4},{6,7},{7,6},{8,9},{9,8},{10,11... | collective-permute-start | bytes 393224 | tf_op jit(solution)/shard_map/ppermute | solution.py:316
  13.2 7.5 %collective-permute-start.2 = (bf16[128,1024]{1,0:T(8,128)(2,1)S(1)}, bf16[128,1024]{1,0:T(8,128)(2,1)S(1)}, u32[]{:S(2)}, u32[]{:S(2)}) collective-permute-start(bf16[128,1024]{1,0:T(8,128)(2,1)S(1)} %get-tuple-element.37), channel_id=1, source_target_pairs={{1,0},{0,1},{3,2},{2,3},{5,4},{4,5},{7,6},{6,7},{9,8},{8,9},{11,10... | collective-permute-start | bytes 786440 | tf_op jit(solution)/shard_map/ppermute | solution.py:319
  14.9 12.0 %all-to-all-start = ((bf16[32,8,128]{2,1,0:T(8,128)(2,1)}), bf16[32,8,128]{2,1,0:T(8,128)(2,1)S(1)}, u32[]{:S(2)}, u32[]{:S(2)}) async-start(bf16[32,8,128]{2,1,0:T(8,128)(2,1)} %get-tuple-element.42), calls=%async_computation | async-start | bytes 131072 | tf_op jit(solution)/shard_map/all_to_all | solution.py:380

commit v6 on v5

--- a/solution.py
+++ b/solution.py
@@ -107,9 +107,10 @@
     return jnp.concatenate([first, x[2 * rows:]], axis=0) if nb > 1 else first
 
 
-def split(near_b, far_b, x, nb):
+def split(near_b, x, nb):
     rows = near_b.shape[0]
-    parts = [x[:rows] * near_b, x[:rows] * far_b]
+    own = x[:rows] * near_b
+    parts = [own, x[:rows] - own]
     if nb > 1:
         parts.append(x[rows:])
     return jnp.concatenate(parts, axis=0)
@@ -154,7 +155,6 @@
     scale = hd ** -0.5
     near = near_mask(rows)
     near_b = near.astype(F32).astype(BF16)
-    far_b = 1.0 - near_b
 
     def k_cols(n):
         return slice(n * hd, (n + 1) * hd)
@@ -177,7 +177,7 @@
 
     def value_grad(n):
         p2 = jnp.concatenate(
-            [split(near_b, far_b, p_ref[:, n * span + h * rows:n * span + (h + 1) * rows], nb) for h in range(heads)],
+            [split(near_b, p_ref[:, n * span + h * rows:n * span + (h + 1) * rows], nb) for h in range(heads)],
             axis=1,
         )
         v_grad = lax.dot_general(gt_ref[k_cols(n), :], p2, ACROSS, preferred_element_type=F32).T
@@ -196,7 +196,7 @@
             delta = jnp.sum(p * dp, axis=0, keepdims=True)
             ds_b = (p * (dp - delta)).astype(BF16)
             ds_ref[:, at] = ds_b
-            ds.append(split(near_b, far_b, ds_b, nb))
+            ds.append(split(near_b, ds_b, nb))
         return jnp.concatenate(ds, axis=1)
 
     def key_side(n, ds2):
@@ -237,7 +237,6 @@
     hd = k2_ref.shape[1] // kv_heads
     heads = group // hd
     near_b = near_mask(rows).astype(F32).astype(BF16)
-    far_b = 1.0 - near_b
 
     def copies(n):
         cols = pl.ds(pl.multiple_of(n * group, group), group)
@@ -252,7 +251,7 @@
             at = pl.ds(pl.multiple_of(n * heads * rows, rows), heads * rows)
             x = right[:, at]
             x2 = jnp.concatenate(
-                [split(near_b, far_b, x[:, h * rows:(h + 1) * rows], nb) for h in range(heads)], axis=1
+                [split(near_b, x[:, h * rows:(h + 1) * rows], nb) for h in range(heads)], axis=1
             )
             y = jnp.dot(left[:, cols].T, x2, preferred_element_type=F32)
             y = (y if scale is None else y * scale).astype(BF16)

time: 27.8 us -> 27.8 us (level)
  no operation moved by 1% of the time
where the time goes in v6:
time: 27.8 us; the launch traced here: 27.6 us
  Pallas kernels  10 us (36%)
  starting transfers between devices  9.74 us (35%)
  waiting for transfers between devices  7.14 us (26%)
  between operations  0.67 us (2%)
    pallas_call x5, Pallas kernels, call(): pl.pallas_call(kernel, out_shape=outs, in_specs=in_specs or [vmem] * len(...  10 us
    all_to_all x1, starting transfers between devices, on_device(): lax.all_to_all(spread, ('dp', 'seq'), split_axis=0, concat_axis=0, axis_i...  4.89 us
    all_to_all x1, waiting for transfers between devices, on_device(): lax.all_to_all(spread, ('dp', 'seq'), split_axis=0, concat_axis=0, axis_i...  3.98 us
    ppermute x2, starting transfers between devices, shift(): lax.ppermute(array, 'seq', [(r, (r + d) % seq_count) for r in range(seq_c...  3.11 us
    ppermute x2, waiting for transfers between devices, shift(): lax.ppermute(array, 'seq', [(r, (r + d) % seq_count) for r in range(seq_c...  2.3 us
    ppermute x1, starting transfers between devices, unshift(): lax.ppermute(array, 'seq', [((r + d) % seq_count, r) for r in range(seq_c...  1.74 us
    ppermute x1, waiting for transfers between devices, unshift(): lax.ppermute(array, 'seq', [((r + d) % seq_count, r) for r in range(seq_c...  0.86 us
  transfers between devices with their start and end apart: 4, of which 4 were waited for; matrix products, arithmetic and copies ran while one was open for 0% of the time, Pallas kernels for 23%

profile of v6, /device:TPU:0, one launch (start us, length us, event | category | flops | bytes accessed | tf_op | source)
XLA Modules:
  0.0 27.6 jit_solution(17829529911599066252)
XLA Ops:
  0.6 3.0 %collective-permute-start = (bf16[128,512]{1,0:T(8,128)(2,1)}, bf16[128,512]{1,0:T(8,128)(2,1)S(1)}, u32[]{:S(2)}, u32[]{:S(2)}) collective-permute-start(bf16[128,512]{1,0:T(8,128)(2,1)} %key_hbm.1), channel_id=1, source_target_pairs={{0,1},{1,0},{2,3},{3,2},{4,5},{5,4},{6,7},{7,6},{8,9},{9,8},{10,11... | collective-permute-start | bytes 393224 | tf_op jit(solution)/shard_map/ppermute | solution.py:315
  3.7 0.1 collective-permute-start.1
  3.7 2.6 %prep.1 = (bf16[512,1024]{1,0:T(8,128)(2,1)S(1)}, bf16[512,1024]{1,0:T(8,128)(2,1)S(1)}, bf16[128,1024]{1,0:T(8,128)(2,1)S(1)}, f32[128,1024]{1,0:T(8,128)}, f32...) custom-call(bf16[128,4096]{1,0:T(8,128)(2,1)} %q_hbm.1, bf16[128,4096]{1,0:T(8,128)(2,1)} %g_hbm.1, ...), custom_call_target="tpu_custom_call" | custom-call | flops 134217728 | bytes 1048576 | tf_op jit(solution)/shard_map/prep/pallas_call | solution.py:303
  6.3 1.9 %collective-permute-done.rest_0_ = bf16[128,512]{1,0:T(8,128)(2,1)S(1)} collective-permute-done((bf16[128,512]{1,0:T(8,128)(2,1)}, bf16[128,512]{1,0:T(8,128)(2,1)S(1)}, u32[]{:S(2)}, u32[]{:S(2)}) %collective-permute-start) | collective-permute-done | bytes 131104 | tf_op jit(solution)/shard_map/ppermute | solution.py:315
  8.2 1.5 %score.1 = (bf16[128,4096]{1,0:T(8,128)(2,1)S(1)}, bf16[256,512]{1,0:T(8,128)(2,1)S(1)}, f32[128,512]{1,0:T(8,128)S(1)}) custom-call(bf16[512,1024]{1,0:T(8,128)(2,1)S(1)} %get-tuple-element.24.qt_ref, bf16[128,1024]{1,0:T(8,128)(2,1)S(1)} %get-tuple-element.25.quant_ref, f32[128,128]{1,0:T(8,128)S(1)} %get-tuple-element.26.bias_ref, ...), custom_call_target="tpu_custom_call" | custom-call | flops 268435456 | bytes 1048576 | tf_op jit(solution)/shard_map/score/pallas_call | solution.py:303
  9.7 0.4 %collective-permute-done.1.rest_0_ = bf16[128,512]{1,0:T(8,128)(2,1)S(1)} collective-permute-done((bf16[128,512]{1,0:T(8,128)(2,1)}, bf16[128,512]{1,0:T(8,128)(2,1)S(1)}, u32[]{:S(2)}, u32[]{:S(2)}) %collective-permute-start.1) | collective-permute-done | bytes 131104 | tf_op jit(solution)/shard_map/ppermute | solution.py:315
  10.2 3.0 %grad.1 = (bf16[128,4096]{1,0:T(8,128)(2,1)S(1)}, bf16[256,512]{1,0:T(8,128)(2,1)S(1)}, bf16[128,1024]{1,0:T(8,128)(2,1)S(1)}, bf16[128,1024]{1,0:T(8,128)(2,1)S(1)}, bf16[32,8,128]{2,1,0:T(8,128)(2,1)}) custom-call(bf16[512,1024]{1,0:T(8,128)(2,1)S(1)} %get-tuple-element.24.qt_ref, bf16[512,1024]{1,0:T(8,128)(2,1)S(1)} %get-tuple-element.29.gt_ref, ...), custom_call_target="tpu_custom_call" | custom-call | flops 805306368 | bytes 1048576 | tf_op jit(solution)/shard_map/grad/pallas_call | solution.py:303
  13.2 1.7 %collective-permute-start.2 = (bf16[128,1024]{1,0:T(8,128)(2,1)S(1)}, bf16[128,1024]{1,0:T(8,128)(2,1)S(1)}, u32[]{:S(2)}, u32[]{:S(2)}) collective-permute-start(bf16[128,1024]{1,0:T(8,128)(2,1)S(1)} %get-tuple-element.37), channel_id=1, source_target_pairs={{1,0},{0,1},{3,2},{2,3},{5,4},{4,5},{7,6},{6,7},{9,8},{8,9},{11,10... | collective-permute-start | bytes 786440 | tf_op jit(solution)/shard_map/ppermute | solution.py:318
  14.9 4.9 %all-to-all-start = ((bf16[32,8,128]{2,1,0:T(8,128)(2,1)}), bf16[32,8,128]{2,1,0:T(8,128)(2,1)S(1)}, u32[]{:S(2)}, u32[]{:S(2)}) async-start(bf16[32,8,128]{2,1,0:T(8,128)(2,1)} %get-tuple-element.42), calls=%async_computation | async-start | bytes 131072 | tf_op jit(solution)/shard_map/all_to_all | solution.py:379
  19.8 0.9 %collective-permute-done.2.rest_0_ = bf16[128,1024]{1,0:T(8,128)(2,1)S(1)} collective-permute-done((bf16[128,1024]{1,0:T(8,128)(2,1)S(1)}, bf16[128,1024]{1,0:T(8,128)(2,1)S(1)}, u32[]{:S(2)}, u32[]{:S(2)}) %collective-permute-start.2) | collective-permute-done | bytes 262176 | tf_op jit(solution)/shard_map/ppermute | solution.py:318
  20.7 2.3 %output.1 = (bf16[128,4096]{1,0:T(8,128)(2,1)}, bf16[128,4096]{1,0:T(8,128)(2,1)}, bf16[128,512]{1,0:T(8,128)(2,1)}, bf16[128,512]{1,0:T(8,128)(2,1)}) custom-call(bf16[128,4096]{1,0:T(8,128)(2,1)S(1)} %get-tuple-element.28.p_ref, bf16[128,4096]{1,0:T(8,128)(2,1)S(1)} %get-tuple-element.32.ds_ref, bf16[256,512]{1,0:T(8,128)(2,1)S(1)} %get-tuple-element.33.k2_ref, ...), custom_call_target="tpu_custom_call" | custom-call | flops 536870912 | bytes 1048576 | tf_op jit(solution)/shard_map/output/pallas_call | solution.py:303
  23.0 4.0 %all-to-all-done.parts_ref = bf16[32,8,128]{2,1,0:T(8,128)(2,1)S(1)} async-done(((bf16[32,8,128]{2,1,0:T(8,128)(2,1)}), bf16[32,8,128]{2,1,0:T(8,128)(2,1)S(1)}, u32[]{:S(2)}, u32[]{:S(2)}) %all-to-all-start) | async-done | bytes 65568 | tf_op jit(solution)/shard_map/all_to_all | solution.py:379
  26.9 0.6 %total.1 = f32[8,128]{1,0:T(8,128)} custom-call(bf16[32,8,128]{2,1,0:T(8,128)(2,1)S(1)} %all-to-all-done.parts_ref, bf16[128,512]{1,0:T(8,128)(2,1)} %get-tuple-element.21.after_ref), custom_call_target="tpu_custom_call" | custom-call | flops 32768 | bytes 1048576 | tf_op jit(solution)/shard_map/total/pallas_call | solution.py:303
Async XLA Ops:
  0.6 7.6 %collective-permute-start = (bf16[128,512]{1,0:T(8,128)(2,1)}, bf16[128,512]{1,0:T(8,128)(2,1)S(1)}, u32[]{:S(2)}, u32[]{:S(2)}) collective-permute-start(bf16[128,512]{1,0:T(8,128)(2,1)} %key_hbm.1), channel_id=1, source_target_pairs={{0,1},{1,0},{2,3},{3,2},{4,5},{5,4},{6,7},{7,6},{8,9},{9,8},{10,11... | collective-permute-start | bytes 393224 | tf_op jit(solution)/shard_map/ppermute | solution.py:315
  3.7 6.5 %collective-permute-start.1 = (bf16[128,512]{1,0:T(8,128)(2,1)}, bf16[128,512]{1,0:T(8,128)(2,1)S(1)}, u32[]{:S(2)}, u32[]{:S(2)}) collective-permute-start(bf16[128,512]{1,0:T(8,128)(2,1)} %value_hbm.1), channel_id=1, source_target_pairs={{0,1},{1,0},{2,3},{3,2},{4,5},{5,4},{6,7},{7,6},{8,9},{9,8},{10,11... | collective-permute-start | bytes 393224 | tf_op jit(solution)/shard_map/ppermute | solution.py:315
  13.2 7.5 %collective-permute-start.2 = (bf16[128,1024]{1,0:T(8,128)(2,1)S(1)}, bf16[128,1024]{1,0:T(8,128)(2,1)S(1)}, u32[]{:S(2)}, u32[]{:S(2)}) collective-permute-start(bf16[128,1024]{1,0:T(8,128)(2,1)S(1)} %get-tuple-element.37), channel_id=1, source_target_pairs={{1,0},{0,1},{3,2},{2,3},{5,4},{4,5},{7,6},{6,7},{9,8},{8,9},{11,10... | collective-permute-start | bytes 786440 | tf_op jit(solution)/shard_map/ppermute | solution.py:318
  14.9 12.0 %all-to-all-start = ((bf16[32,8,128]{2,1,0:T(8,128)(2,1)}), bf16[32,8,128]{2,1,0:T(8,128)(2,1)S(1)}, u32[]{:S(2)}, u32[]{:S(2)}) async-start(bf16[32,8,128]{2,1,0:T(8,128)(2,1)} %get-tuple-element.42), calls=%async_computation | async-start | bytes 131072 | tf_op jit(solution)/shard_map/all_to_all | solution.py:379
